TPU v7x, 32 devices: a whole 2x2x4 slice. The times are simulated.
32 devices in a mesh: fsdp: 2 (over x), ctx: 4 (over y, core), head: 4 (over z).
Axes of the slice: x: 2, y: 2, z: 4, core: 2. Of those that a mesh axis runs over, the one named last changes fastest.
Arguments:
- tokens: bfloat16 [4096, 4, 768], P(('ctx', 'head'), 'fsdp'), may hold values from -6 to 6
- segment_ids: int32 [4, 4096], P('fsdp', 'ctx'), may hold values from 0 to 4095, as said below
- routes: int32 [16, 2, 512, 2], P(('ctx', 'head'), 'fsdp'), may hold values from 0 to 3, all different within a row; in each aligned block of 512 rows (0 to 511, 512 to 1023, ..., all dimensions but the last counted through in order) at most 384 rows name the same one
- cotangent: bfloat16 [4096, 4, 768], P(('ctx', 'head'), 'fsdp'), may hold values from -6 to 6
- norm1_gain: bfloat16 [768], P('fsdp'), may hold values from 0.25 to 1.75
- qkv_weight: bfloat16 [768, 2304], P('fsdp'), may hold values from -0.21875 to 0.21875
- out_weight: bfloat16 [768, 768], P('fsdp'), may hold values from -0.875 to 0.875
- norm2_gain: bfloat16 [768], P('fsdp'), may hold values from 0.25 to 1.75
- router_weight: bfloat16 [768, 4], P('fsdp'), may hold values from -0.15625 to 0.15625
- shared_in: bfloat16 [768, 4096], P('fsdp'), may hold values from -0.21875 to 0.21875
- shared_out: bfloat16 [2048, 768], P('fsdp'), may hold values from -0.125 to 0.125
- expert_in: bfloat16 [4, 768, 4096], P(None, 'fsdp'), may hold values from -0.21875 to 0.21875
- expert_out: bfloat16 [4, 2048, 768], P(None, 'fsdp'), may hold values from -0.125 to 0.125
Outputs:
- output: bfloat16 [4096, 4, 768], P(('ctx', 'head'), 'fsdp')
- tokens_grad: float32 [4096, 4, 768], P(('ctx', 'head'), 'fsdp')
- norm1_gain_grad: float32 [768], P('fsdp')
- qkv_weight_grad: float32 [768, 2304], P('fsdp')
- out_weight_grad: float32 [768, 768], P('fsdp')
- norm2_gain_grad: float32 [768], P('fsdp')
- router_weight_grad: float32 [768, 4], P('fsdp')
- shared_in_grad: float32 [768, 4096], P('fsdp')
- shared_out_grad: float32 [2048, 768], P('fsdp')
- expert_in_grad: float32 [4, 768, 4096], P(None, 'fsdp')
- expert_out_grad: float32 [4, 2048, 768], P(None, 'fsdp')
Inputs may be any that keep to these rules, and one draw needn't show every extreme that they name: `segment_ids`: each entry is the position in its sequence at which its document starts, so entries never fall along a sequence and each sequence begins with 0. `routes`: each token names two different experts. Among the rows of one device no expert is named more than 384 times, and in every draw some device's rows name one expert exactly 384 times.
All inputs are finite; a program needn't handle non-finite values.
Results may differ from a plain program's by a relative error of at most 0.023.
Values may be sent and summed in bfloat16 or wider, within the bound.
A program may use at most 256 MiB of HBM per device.

v0:
```python
import math

import jax
import jax.numpy as jnp
from jax import lax
from jax.sharding import PartitionSpec as P

HEAD_DIM = 64
FF = 2048
FS = 2048
EXPERTS = 4
CAP = 384


EPS = 1e-06
NEG = -1e30
ROPE_BASE = 10000.0


def rms_norm(values, gain):
    return values * lax.rsqrt(jnp.mean(values * values, axis=-1, keepdims=True) + EPS) * gain


def rotate(values, position):
    half_dim = values.shape[-1] // 2
    freq_index = jnp.arange(half_dim).astype(jnp.float32)
    freq_table = jnp.exp(-math.log(ROPE_BASE) * 2.0 * freq_index / values.shape[-1])
    angle_table = position.astype(jnp.float32)[:, None] * freq_table[None, :]
    cosine = jnp.cos(angle_table)[:, None, :]
    sine_part = jnp.sin(angle_table)[:, None, :]
    first_half = values[..., :half_dim]
    second_half = values[..., half_dim:]
    return jnp.concatenate(
        [
            first_half * cosine - second_half * sine_part,
            second_half * cosine + first_half * sine_part,
        ],
        axis=-1,
    )


def swiglu(values, hidden_width):
    gate_part = values[..., :hidden_width]
    return gate_part * jax.nn.sigmoid(gate_part) * values[..., hidden_width:]


def softmax_rows(values):
    row_top = jnp.max(values, axis=-1, keepdims=True)
    weights = jnp.exp(values - row_top)
    return weights / jnp.sum(weights, axis=-1, keepdims=True)


def mix_weights(logits, route_rows):
    router_prob = softmax_rows(logits)
    picked = (route_rows[:, :, None] == jnp.arange(logits.shape[-1])[None, None, :]).astype(
        logits.dtype
    )
    chosen = jnp.sum(router_prob[:, None, :] * picked, axis=-1)
    gate_value = chosen / jnp.sum(chosen, axis=-1, keepdims=True)
    return jnp.sum(gate_value[:, :, None] * picked, axis=1)


def left_dot(first, second):
    return lax.dot_general(
        first, second, (((0,), (0,)), ((), ())), preferred_element_type=jnp.float32
    )


def right_dot(first, second):
    return lax.dot_general(
        first, second, (((1,), (1,)), ((), ())), preferred_element_type=jnp.float32
    )


def make_scorer(queries, keys_head, query_marks, key_marks, query_pos, block_len):
    score_scale = HEAD_DIM ** (-0.5)

    def scorer(block_index):
        start = block_index * block_len
        key_block = lax.dynamic_slice_in_dim(keys_head, start, block_len, 1)
        key_pos = start + jnp.arange(block_len, dtype=jnp.int32)
        block_marks = lax.dynamic_slice_in_dim(key_marks, start, block_len, 0)
        scores = (
            jnp.einsum("hqd,hkd->hqk", queries, key_block, preferred_element_type=jnp.float32)
            * score_scale
        )
        visible = (key_pos[None, :] <= query_pos[:, None]) & (
            block_marks[None, :] == query_marks[:, None]
        )
        return (scores, visible[None], key_block)

    return scorer


def attend_forward(item_data, query_pos, block_len, block_limit):
    queries, keys_head, values_head, query_marks, key_marks = item_data
    scorer = make_scorer(queries, keys_head, query_marks, key_marks, query_pos, block_len)

    def stats_step(block_index, carry):
        row_top, row_total = carry
        scores, visible, _ = scorer(block_index)
        new_top = jnp.maximum(row_top, jnp.max(jnp.where(visible, scores, NEG), axis=-1))
        row_total = row_total * jnp.exp(row_top - new_top) + jnp.sum(
            jnp.where(visible, jnp.exp(scores - new_top[..., None]), 0.0), axis=-1
        )
        return (new_top, row_total)

    start_top = jnp.full(queries.shape[:2], NEG, jnp.float32)
    row_top, row_total = lax.fori_loop(
        0, block_limit, stats_step, (start_top, jnp.zeros(queries.shape[:2], jnp.float32))
    )
    log_total = row_top + jnp.log(row_total)

    def value_step(block_index, accum):
        scores, visible, _ = scorer(block_index)
        weights = jnp.where(visible, jnp.exp(scores - log_total[..., None]), 0.0).astype(
            jnp.bfloat16
        )
        value_block = lax.dynamic_slice_in_dim(values_head, block_index * block_len, block_len, 1)
        return accum + jnp.einsum(
            "hqk,hkd->hqd", weights, value_block, preferred_element_type=jnp.float32
        )

    attended = lax.fori_loop(0, block_limit, value_step, jnp.zeros(queries.shape, jnp.float32))
    return (attended, log_total)


def attend_backward(item_data, query_pos, block_len, block_limit):
    queries, keys_head, values_head, query_marks, key_marks, grad_out, attended, log_total = (
        item_data
    )
    score_scale = HEAD_DIM ** (-0.5)
    scorer = make_scorer(queries, keys_head, query_marks, key_marks, query_pos, block_len)
    row_delta = jnp.sum(grad_out.astype(jnp.float32) * attended, axis=-1)

    def grad_step(block_index, carry):
        grad_query, grad_keys, grad_values = carry
        scores, visible, key_block = scorer(block_index)
        start = block_index * block_len
        value_block = lax.dynamic_slice_in_dim(values_head, start, block_len, 1)
        weights = jnp.where(visible, jnp.exp(scores - log_total[..., None]), 0.0)
        grad_weights = jnp.einsum(
            "hqd,hkd->hqk", grad_out, value_block, preferred_element_type=jnp.float32
        )
        grad_scores = (weights * (grad_weights - row_delta[..., None]) * score_scale).astype(
            jnp.bfloat16
        )
        grad_query = grad_query + jnp.einsum(
            "hqk,hkd->hqd", grad_scores, key_block, preferred_element_type=jnp.float32
        )
        key_part = jnp.einsum(
            "hqk,hqd->hkd", grad_scores, queries, preferred_element_type=jnp.float32
        )
        value_part = jnp.einsum(
            "hqk,hqd->hkd",
            weights.astype(jnp.bfloat16),
            grad_out,
            preferred_element_type=jnp.float32,
        )
        grad_keys = lax.dynamic_update_slice_in_dim(grad_keys, key_part, start, 1)
        grad_values = lax.dynamic_update_slice_in_dim(grad_values, value_part, start, 1)
        return (grad_query, grad_keys, grad_values)

    start_carry = (
        jnp.zeros(queries.shape, jnp.float32),
        jnp.zeros(keys_head.shape, jnp.float32),
        jnp.zeros(keys_head.shape, jnp.float32),
    )
    return lax.fori_loop(0, block_limit, grad_step, start_carry)


def on_device(
    tokens,
    segment_ids,
    routes,
    cotangent,
    norm1_gain,
    qkv_weight,
    out_weight,
    norm2_gain,
    router_weight,
    shared_in,
    shared_out,
    expert_in,
    expert_out,
):
    local_len, seq_count, model_width = tokens.shape
    row_count = local_len * seq_count
    head_count = model_width // HEAD_DIM
    head_groups = lax.axis_size("head")
    local_heads = head_count // head_groups
    group_width = local_heads * HEAD_DIM
    ctx_count = lax.axis_size("ctx")
    ctx_index = lax.axis_index("ctx")
    head_index = lax.axis_index("head")
    block_len = local_len * head_groups
    seq_len = block_len * ctx_count
    block_limit = ctx_index + 1
    token_rows = tokens.reshape(row_count, model_width).astype(jnp.float32)
    grad_rows = cotangent.reshape(row_count, model_width).astype(jnp.float32)
    route_rows = routes.reshape(row_count, 2)
    dense_full = (
        lax.all_gather(norm1_gain, "fsdp", axis=0, tiled=True),
        lax.all_gather(qkv_weight, "fsdp", axis=0, tiled=True),
        lax.all_gather(out_weight, "fsdp", axis=0, tiled=True),
        lax.all_gather(norm2_gain, "fsdp", axis=0, tiled=True),
        lax.all_gather(router_weight, "fsdp", axis=0, tiled=True),
        lax.all_gather(shared_in, "fsdp", axis=0, tiled=True),
        lax.all_gather(shared_out, "fsdp", axis=0, tiled=True),
    )
    norm_one, w_qkv, w_attn, norm_two, w_router, w_shared_in, w_shared_out = dense_full
    norm_one = norm_one.astype(jnp.float32)
    norm_two = norm_two.astype(jnp.float32)
    local_pos = (ctx_index * head_groups + head_index) * local_len + jnp.arange(
        local_len, dtype=jnp.int32
    )
    row_pos = jnp.broadcast_to(local_pos[:, None], (local_len, seq_count)).reshape(row_count)
    normed = rms_norm(token_rows, norm_one).astype(jnp.bfloat16)
    mixed_qkv = jnp.dot(normed, w_qkv, preferred_element_type=jnp.float32)
    rotated = rotate(
        mixed_qkv[:, : 2 * model_width].reshape(row_count, 2 * head_count, HEAD_DIM), row_pos
    )
    outgoing = jnp.concatenate(
        [rotated.reshape(row_count, 2 * model_width), mixed_qkv[:, 2 * model_width :]], axis=1
    ).astype(jnp.bfloat16)
    outgoing = outgoing.reshape(local_len, seq_count, 3, head_groups, group_width)
    incoming = lax.all_to_all(outgoing, "head", split_axis=3, concat_axis=0, tiled=True)
    query_head = (
        incoming[:, :, 0, 0]
        .reshape(block_len, seq_count, local_heads, HEAD_DIM)
        .transpose(1, 2, 0, 3)
    )
    key_value = incoming[:, :, 1:, 0]
    marks_local = segment_ids.T
    key_value_all, marks_all = (
        lax.all_gather(key_value, "ctx", axis=0, tiled=True),
        lax.all_gather(marks_local, "ctx", axis=0, tiled=True),
    )
    key_head = (
        key_value_all[:, :, 0]
        .reshape(seq_len, seq_count, local_heads, HEAD_DIM)
        .transpose(1, 2, 0, 3)
    )
    value_head = (
        key_value_all[:, :, 1]
        .reshape(seq_len, seq_count, local_heads, HEAD_DIM)
        .transpose(1, 2, 0, 3)
    )
    key_marks = marks_all.T
    query_pos = ctx_index * block_len + jnp.arange(block_len, dtype=jnp.int32)
    attended, log_total = lax.map(
        lambda item_data: attend_forward(item_data, query_pos, block_len, block_limit),
        (query_head, key_head, value_head, segment_ids, key_marks),
    )
    returning = (
        attended.astype(jnp.bfloat16)
        .transpose(2, 0, 1, 3)
        .reshape(block_len, seq_count, 1, group_width)
    )
    attn_back = lax.all_to_all(returning, "head", split_axis=0, concat_axis=2, tiled=True)
    attn_rows = attn_back.reshape(row_count, model_width)
    hidden = token_rows + jnp.dot(attn_rows, w_attn, preferred_element_type=jnp.float32)
    normed_two = rms_norm(hidden, norm_two).astype(jnp.bfloat16)
    logits = jnp.dot(normed_two, w_router, preferred_element_type=jnp.float32)
    mixing = mix_weights(logits, route_rows)
    shared_pre = jnp.dot(normed_two, w_shared_in, preferred_element_type=jnp.float32)
    shared_act = swiglu(shared_pre, FS).astype(jnp.bfloat16)
    shared_result = jnp.dot(shared_act, w_shared_out, preferred_element_type=jnp.float32)
    expert_ids = jnp.arange(EXPERTS, dtype=jnp.int32)
    member = jnp.sum(
        (route_rows[:, :, None] == expert_ids[None, None, :]).astype(jnp.int32), axis=1
    )
    slot_rank = jnp.cumsum(member, axis=0) - 1
    target = jnp.where(member > 0, slot_rank, CAP)
    expert_grid = jnp.broadcast_to(expert_ids[None, :], (row_count, EXPERTS))
    row_grid = jnp.broadcast_to(
        jnp.arange(row_count, dtype=jnp.int32)[:, None], (row_count, EXPERTS)
    )
    slot_rows = (
        jnp.zeros((EXPERTS, CAP), jnp.int32).at[expert_grid, target].set(row_grid, mode="drop")
    )
    slot_used = jnp.zeros((EXPERTS, CAP), jnp.float32).at[expert_grid, target].set(1.0, mode="drop")
    slot_gate = mixing[slot_rows, expert_ids[:, None]] * slot_used
    dispatched = normed_two[slot_rows]
    slot_grad_rows = grad_rows[slot_rows]
    grad_results = (slot_gate[..., None] * slot_grad_rows).astype(jnp.bfloat16)

    def expert_forward(carry, item_data):
        local_in, local_out, rows_in = item_data
        full_in, full_out = (
            lax.all_gather(local_in, "fsdp", axis=0, tiled=True),
            lax.all_gather(local_out, "fsdp", axis=0, tiled=True),
        )
        expert_pre = jnp.dot(rows_in, full_in, preferred_element_type=jnp.float32)
        expert_act = swiglu(expert_pre, FF).astype(jnp.bfloat16)
        expert_result = jnp.dot(expert_act, full_out, preferred_element_type=jnp.float32)
        stored = ()
        return (carry, (expert_result, stored))

    _, (expert_results, stored_experts) = lax.scan(
        expert_forward, None, (expert_in, expert_out, dispatched)
    )
    combined = (
        jnp.zeros((row_count, model_width), jnp.float32)
        .at[slot_rows.reshape(-1)]
        .add((slot_gate[..., None] * expert_results).reshape(-1, model_width))
    )
    result = hidden + shared_result + combined
    output = result.astype(jnp.bfloat16).reshape(local_len, seq_count, model_width)
    back_dense = (
        lax.all_gather(norm1_gain, "fsdp", axis=0, tiled=True),
        lax.all_gather(qkv_weight, "fsdp", axis=0, tiled=True),
        lax.all_gather(out_weight, "fsdp", axis=0, tiled=True),
        lax.all_gather(norm2_gain, "fsdp", axis=0, tiled=True),
        lax.all_gather(router_weight, "fsdp", axis=0, tiled=True),
        lax.all_gather(shared_in, "fsdp", axis=0, tiled=True),
        lax.all_gather(shared_out, "fsdp", axis=0, tiled=True),
    )
    _, w_qkv, w_attn, _, w_router, w_shared_in, w_shared_out = back_dense
    grad_low = grad_rows.astype(jnp.bfloat16)
    shared_out_grad = left_dot(shared_act, grad_low)
    _, shared_pull = jax.vjp(lambda values: swiglu(values, FS), shared_pre)
    grad_shared_pre = shared_pull(right_dot(grad_low, w_shared_out))[0].astype(jnp.bfloat16)
    shared_in_grad = left_dot(normed_two, grad_shared_pre)
    grad_normed = right_dot(grad_shared_pre, w_shared_in)
    grad_mix_slots = jnp.sum(slot_grad_rows * expert_results, axis=-1) * slot_used
    grad_mixing = (
        jnp.zeros((row_count, EXPERTS), jnp.float32)
        .at[slot_rows, expert_ids[:, None]]
        .add(grad_mix_slots)
    )

    def expert_backward(carry, item_data):
        local_in, local_out, rows_in, grad_out_rows, stored = item_data
        full_in, full_out = (
            lax.all_gather(local_in, "fsdp", axis=0, tiled=True),
            lax.all_gather(local_out, "fsdp", axis=0, tiled=True),
        )
        expert_pre = jnp.dot(rows_in, full_in, preferred_element_type=jnp.float32)
        expert_act, act_pull = jax.vjp(lambda values: swiglu(values, FF), expert_pre)
        out_grad = left_dot(expert_act.astype(jnp.bfloat16), grad_out_rows)
        grad_pre = act_pull(right_dot(grad_out_rows, full_out))[0].astype(jnp.bfloat16)
        in_grad = left_dot(rows_in, grad_pre)
        grad_rows_in = right_dot(grad_pre, full_in)
        in_share, out_share = (
            lax.psum_scatter(
                in_grad.astype(jnp.bfloat16), "fsdp", scatter_dimension=0, tiled=True
            ).astype(jnp.float32),
            lax.psum_scatter(
                out_grad.astype(jnp.bfloat16), "fsdp", scatter_dimension=0, tiled=True
            ).astype(jnp.float32),
        )
        return (carry, (grad_rows_in, in_share, out_share))

    _, (grad_dispatched, expert_in_share, expert_out_share) = lax.scan(
        expert_backward, None, (expert_in, expert_out, dispatched, grad_results, stored_experts)
    )
    grad_normed = grad_normed + jnp.zeros((row_count, model_width), jnp.float32).at[
        slot_rows.reshape(-1)
    ].add(grad_dispatched.reshape(-1, model_width))
    _, mix_pull = jax.vjp(lambda values: mix_weights(values, route_rows), logits)
    grad_logits = mix_pull(grad_mixing)[0].astype(jnp.bfloat16)
    router_grad = left_dot(normed_two, grad_logits)
    grad_normed = grad_normed + right_dot(grad_logits, w_router)
    _, second_pull = jax.vjp(rms_norm, hidden, norm_two)
    grad_hidden_part, norm_two_grad = second_pull(grad_normed)
    grad_hidden = grad_rows + grad_hidden_part
    grad_hidden_low = grad_hidden.astype(jnp.bfloat16)
    attn_grad = left_dot(attn_rows, grad_hidden_low)
    grad_attn = (
        right_dot(grad_hidden_low, w_attn)
        .astype(jnp.bfloat16)
        .reshape(local_len, seq_count, head_groups, group_width)
    )
    grad_head = lax.all_to_all(grad_attn, "head", split_axis=2, concat_axis=0, tiled=True)
    grad_out = grad_head.reshape(block_len, seq_count, local_heads, HEAD_DIM).transpose(1, 2, 0, 3)
    grad_query, grad_keys, grad_values = lax.map(
        lambda item_data: attend_backward(item_data, query_pos, block_len, block_limit),
        (query_head, key_head, value_head, segment_ids, key_marks, grad_out, attended, log_total),
    )
    key_terms = (
        jnp.stack([grad_keys, grad_values], axis=2)
        .transpose(3, 0, 2, 1, 4)
        .reshape(seq_len, seq_count, 2, group_width)
    )
    key_share = lax.psum_scatter(
        key_terms.astype(jnp.bfloat16), "ctx", scatter_dimension=0, tiled=True
    )
    query_low = (
        grad_query.astype(jnp.bfloat16)
        .transpose(2, 0, 1, 3)
        .reshape(block_len, seq_count, 1, group_width)
    )
    sending = jnp.concatenate([query_low, key_share], axis=2)[:, :, :, None, :]
    grad_local = lax.all_to_all(sending, "head", split_axis=0, concat_axis=3, tiled=True)
    grad_local = grad_local.reshape(row_count, 3, model_width).astype(jnp.float32)
    grad_rotated = grad_local[:, :2].reshape(row_count, 2 * head_count, HEAD_DIM)
    _, rope_pull = jax.vjp(lambda values: rotate(values, row_pos), grad_rotated)
    grad_pairs = rope_pull(grad_rotated)[0].reshape(row_count, 2 * model_width)
    grad_qkv = jnp.concatenate([grad_pairs, grad_local[:, 2]], axis=1).astype(jnp.bfloat16)
    qkv_grad = left_dot(normed, grad_qkv)
    grad_normed_one = right_dot(grad_qkv, w_qkv)
    _, first_pull = jax.vjp(rms_norm, token_rows, norm_one)
    grad_tokens_part, norm_one_grad = first_pull(grad_normed_one)
    tokens_grad = (grad_hidden + grad_tokens_part).reshape(local_len, seq_count, model_width)
    dense_shares = (
        lax.psum_scatter(
            norm_one_grad.astype(jnp.bfloat16), "fsdp", scatter_dimension=0, tiled=True
        ).astype(jnp.float32),
        lax.psum_scatter(
            qkv_grad.astype(jnp.bfloat16), "fsdp", scatter_dimension=0, tiled=True
        ).astype(jnp.float32),
        lax.psum_scatter(
            attn_grad.astype(jnp.bfloat16), "fsdp", scatter_dimension=0, tiled=True
        ).astype(jnp.float32),
        lax.psum_scatter(
            norm_two_grad.astype(jnp.bfloat16), "fsdp", scatter_dimension=0, tiled=True
        ).astype(jnp.float32),
        lax.psum_scatter(
            router_grad.astype(jnp.bfloat16), "fsdp", scatter_dimension=0, tiled=True
        ).astype(jnp.float32),
        lax.psum_scatter(
            shared_in_grad.astype(jnp.bfloat16), "fsdp", scatter_dimension=0, tiled=True
        ).astype(jnp.float32),
        lax.psum_scatter(
            shared_out_grad.astype(jnp.bfloat16), "fsdp", scatter_dimension=0, tiled=True
        ).astype(jnp.float32),
    )
    totals = (
        lax.psum(dense_shares[0].astype(jnp.bfloat16), ("ctx", "head")).astype(jnp.float32),
        lax.psum(dense_shares[1].astype(jnp.bfloat16), ("ctx", "head")).astype(jnp.float32),
        lax.psum(dense_shares[2].astype(jnp.bfloat16), ("ctx", "head")).astype(jnp.float32),
        lax.psum(dense_shares[3].astype(jnp.bfloat16), ("ctx", "head")).astype(jnp.float32),
        lax.psum(dense_shares[4].astype(jnp.bfloat16), ("ctx", "head")).astype(jnp.float32),
        lax.psum(dense_shares[5].astype(jnp.bfloat16), ("ctx", "head")).astype(jnp.float32),
        lax.psum(dense_shares[6].astype(jnp.bfloat16), ("ctx", "head")).astype(jnp.float32),
        lax.psum(expert_in_share.astype(jnp.bfloat16), ("ctx", "head")).astype(jnp.float32),
        lax.psum(expert_out_share.astype(jnp.bfloat16), ("ctx", "head")).astype(jnp.float32),
    )
    return (
        output,
        tokens_grad,
        totals[0],
        totals[1],
        totals[2],
        totals[3],
        totals[4],
        totals[5],
        totals[6],
        totals[7],
        totals[8],
    )


def solution(mesh):
    placed = (
        P(("ctx", "head"), "fsdp", None),
        P("fsdp", "ctx"),
        P(("ctx", "head"), "fsdp", None, None),
        P(("ctx", "head"), "fsdp", None),
        P("fsdp"),
        P("fsdp", None),
        P("fsdp", None),
        P("fsdp"),
        P("fsdp", None),
        P("fsdp", None),
        P("fsdp", None),
        P(None, "fsdp", None),
        P(None, "fsdp", None),
    )
    return jax.shard_map(
        on_device,
        mesh=mesh,
        in_specs=placed,
        out_specs=(
            P(("ctx", "head"), "fsdp", None),
            P(("ctx", "head"), "fsdp", None),
            P("fsdp"),
            P("fsdp", None),
            P("fsdp", None),
            P("fsdp"),
            P("fsdp", None),
            P("fsdp", None),
            P("fsdp", None),
            P(None, "fsdp", None),
            P(None, "fsdp", None),
        ),
        check_vma=False,
    )
```

profile of v0, /device:TPU:1, one launch (start us, length us, event | category | flops | bytes accessed | tf_op | source)
XLA Modules:
  0.0 3139.9 jit_solution(14116373087056338994)
XLA Ops:
  15.7 45.3 %all-gather.29.cloned.1.call-done = bf16[768,2304]{1,0:T(8,128)(2,1)} async-done(((bf16[384,2304]{1,0:T(8,128)(2,1)}), bf16[768,2304]{1,0:T(8,128)(2,1)}) %all-gather.29.cloned.1.call-update) | async-done | bytes 3538960 | tf_op jit(solution)/shard_map/all_gather | solution.py:204
  84.3 57.3 %all_to_all.57 = bf16[256,2,3,4,192]{0,4,2,1,3:T(8,128)(2,1)S(1)} all-to-all(bf16[256,2,3,4,192]{0,4,2,1,3:T(8,128)(2,1)} %copy.179), channel_id=1, replica_groups=mesh['fsdp'=2,'ctx'=4,'head'=4] {'head'}, dimensions={3} | all-to-all | bytes 4718592 | tf_op jit(solution)/shard_map/all_to_all | solution.py:227
  196.0 77.0 %while.105 = (s32[]{:T(128)}, f32[2,3,1024,64]{2,3,1,0:T(8,128)}, f32[2,3,1024]{2,1,0:T(4,128)S(1)}, bf16[2,3,4096,64]{2,3,1,0:T(8,128)(2,1)}, s32[2,4096]{1,0:T...) while((s32[]{:T(128)}, f32[2,3,1024,64]{2,3,1,0:T(8,128)}, ...), condition=%wide.region_8.9_spmd.clone.clone, body=%wide.region_1.8_spmd.clone.sunk.clone | while | flops 1249062912 | bytes 60528516 | solution.py:251
  313.3 612.9 %while.101 = (s32[]{:T(128)}, f32[4,384,768]{2,1,0:T(8,128)}, bf16[4,384,768]{2,1,0:T(8,128)(2,1)S(1)}, bf16[4,384,4096]{2,1,0:T(8,128)(2,1)}, bf16[4,1024,768]{2,1,0:T(8,128)(2,1)}) while((s32[]{:T(128)}, f32[4,384,768]{2,1,0:T(8,128)}, bf16[4,384,768]{2,1,0:T(8,128)(2,1)S(1)}, bf16[4,384,4096]{2,1,0:T(8,128)(2,1)}, ...), condition=%wide.region_21.22_spmd.clone, body=%wide.region_20.21_spmd.sunk.clone | while | flops 3628597248 | bytes 75694240 | solution.py:300
  320.0 137.9 %all-gather.41.cloned.1.call-done = bf16[1,768,4096]{2,1,0:T(8,128)(2,1)} async-done(((bf16[1,384,4096]{2,1,0:T(8,128)(2,1)}), bf16[1,768,4096]{2,1,0:T(8,128)(2,1)}) %all-gather.41.cloned.1.call-update) | async-done | bytes 6291472 | tf_op jit(solution)/shard_map/while/body/eval_jaxpr/all_gather | solution.py:291
  518.2 77.8 %all-gather.41.cloned.1.call-done = bf16[1,768,4096]{2,1,0:T(8,128)(2,1)} async-done(((bf16[1,384,4096]{2,1,0:T(8,128)(2,1)}), bf16[1,768,4096]{2,1,0:T(8,128)(2,1)}) %all-gather.41.cloned.1.call-update) | async-done | bytes 6291472 | tf_op jit(solution)/shard_map/while/body/eval_jaxpr/all_gather | solution.py:291
  656.4 77.8 %all-gather.41.cloned.1.call-done = bf16[1,768,4096]{2,1,0:T(8,128)(2,1)} async-done(((bf16[1,384,4096]{2,1,0:T(8,128)(2,1)}), bf16[1,768,4096]{2,1,0:T(8,128)(2,1)}) %all-gather.41.cloned.1.call-update) | async-done | bytes 6291472 | tf_op jit(solution)/shard_map/while/body/eval_jaxpr/all_gather | solution.py:291
  794.6 77.8 %all-gather.41.cloned.1.call-done = bf16[1,768,4096]{2,1,0:T(8,128)(2,1)} async-done(((bf16[1,384,4096]{2,1,0:T(8,128)(2,1)}), bf16[1,768,4096]{2,1,0:T(8,128)(2,1)}) %all-gather.41.cloned.1.call-update) | async-done | bytes 6291472 | tf_op jit(solution)/shard_map/while/body/eval_jaxpr/all_gather | solution.py:291
  1070.4 1041.9 %while.102 = (s32[]{:T(128)}, f32[4,384,768]{2,1,0:T(8,128)}, bf16[4,384,4096]{2,1,0:T(8,128)(2,1)}, bf16[4,1024,768]{2,1,0:T(8,128)(2,1)}, bf16[4,384,768]{2,1,...) while((s32[]{:T(128)}, f32[4,384,768]{2,1,0:T(8,128)}, ...), condition=%wide.region_34.35_spmd.clone, body=%wide.region_31.34_spmd.sunk.clone | while | flops 9691201536 | bytes 225313120 | solution.py:355
  1077.4 77.8 %all-gather.43.cloned.1.call-done = bf16[1,768,4096]{2,1,0:T(8,128)(2,1)} async-done(((bf16[1,384,4096]{2,1,0:T(8,128)(2,1)}), bf16[1,768,4096]{2,1,0:T(8,128)(2,1)}) %all-gather.43.cloned.1.call-update) | async-done | bytes 6291472 | tf_op jit(solution)/shard_map/while/body/eval_jaxpr/all_gather | solution.py:336
  1249.8 77.2 %reduce-scatter.23.cloned.1.call-done = bf16[384,4096]{1,0:T(8,128)(2,1)} async-done(((bf16[768,4096]{1,0:T(8,128)(2,1)}), bf16[384,4096]{1,0:T(8,128)(2,1)}) %reduce-scatter.23.cloned.1.call-update) | async-done | bytes 3145744 | tf_op jit(solution)/shard_map/while/body/eval_jaxpr/reduce_scatter | solution.py:346
  1337.6 77.8 %all-gather.43.cloned.1.call-done = bf16[1,768,4096]{2,1,0:T(8,128)(2,1)} async-done(((bf16[1,384,4096]{2,1,0:T(8,128)(2,1)}), bf16[1,768,4096]{2,1,0:T(8,128)(2,1)}) %all-gather.43.cloned.1.call-update) | async-done | bytes 6291472 | tf_op jit(solution)/shard_map/while/body/eval_jaxpr/all_gather | solution.py:336
  1510.1 77.3 %reduce-scatter.23.cloned.1.call-done = bf16[384,4096]{1,0:T(8,128)(2,1)} async-done(((bf16[768,4096]{1,0:T(8,128)(2,1)}), bf16[384,4096]{1,0:T(8,128)(2,1)}) %reduce-scatter.23.cloned.1.call-update) | async-done | bytes 3145744 | tf_op jit(solution)/shard_map/while/body/eval_jaxpr/reduce_scatter | solution.py:346
  1598.1 77.8 %all-gather.43.cloned.1.call-done = bf16[1,768,4096]{2,1,0:T(8,128)(2,1)} async-done(((bf16[1,384,4096]{2,1,0:T(8,128)(2,1)}), bf16[1,768,4096]{2,1,0:T(8,128)(2,1)}) %all-gather.43.cloned.1.call-update) | async-done | bytes 6291472 | tf_op jit(solution)/shard_map/while/body/eval_jaxpr/all_gather | solution.py:336
  1770.6 77.3 %reduce-scatter.23.cloned.1.call-done = bf16[384,4096]{1,0:T(8,128)(2,1)} async-done(((bf16[768,4096]{1,0:T(8,128)(2,1)}), bf16[384,4096]{1,0:T(8,128)(2,1)}) %reduce-scatter.23.cloned.1.call-update) | async-done | bytes 3145744 | tf_op jit(solution)/shard_map/while/body/eval_jaxpr/reduce_scatter | solution.py:346
  1858.6 77.8 %all-gather.43.cloned.1.call-done = bf16[1,768,4096]{2,1,0:T(8,128)(2,1)} async-done(((bf16[1,384,4096]{2,1,0:T(8,128)(2,1)}), bf16[1,768,4096]{2,1,0:T(8,128)(2,1)}) %all-gather.43.cloned.1.call-update) | async-done | bytes 6291472 | tf_op jit(solution)/shard_map/while/body/eval_jaxpr/all_gather | solution.py:336
  2031.1 77.3 %reduce-scatter.23.cloned.1.call-done = bf16[384,4096]{1,0:T(8,128)(2,1)} async-done(((bf16[768,4096]{1,0:T(8,128)(2,1)}), bf16[384,4096]{1,0:T(8,128)(2,1)}) %reduce-scatter.23.cloned.1.call-update) | async-done | bytes 3145744 | tf_op jit(solution)/shard_map/while/body/eval_jaxpr/reduce_scatter | solution.py:346
  2159.6 119.6 %while.107 = (s32[]{:T(128)}, bf16[2,3,1024,64]{2,3,1,0:T(8,128)(2,1)}, bf16[2,3,4096,64]{2,3,1,0:T(8,128)(2,1)}, bf16[2,3,4096,64]{2,3,1,0:T(8,128)(2,1)}, bf16...) while((s32[]{:T(128)}, ...), condition=%wide.region_41.42_spmd.clone.clone, body=%wide.region_37.41_spmd.clone.sunk.clone | while | flops 2051800064 | bytes 157533008 | solution.py:377
  2172.2 42.6 %while.106 = (s32[]{:T(128)}, f32[3,1024,64]{1,2,0:T(8,128)S(1)}, bf16[3,4096,64]{1,2,0:T(8,128)(2,1)}, bf16[3,4096,64]{1,2,0:T(8,128)(2,1)}, s32[]{:T(128)}, /*...) while((s32[]{:T(128)}, f32[3,1024,64]{1,2,0:T(8,128)S(1)}, ...), condition=%wide.region_40.40_spmd, body=%wide.region_39.39_spmd.sunk | while | flops 2051212288 | bytes 130318760 | solution.py:169
  2231.8 42.6 %while.106 = (s32[]{:T(128)}, f32[3,1024,64]{1,2,0:T(8,128)S(1)}, bf16[3,4096,64]{1,2,0:T(8,128)(2,1)}, bf16[3,4096,64]{1,2,0:T(8,128)(2,1)}, s32[]{:T(128)}, /*...) while((s32[]{:T(128)}, f32[3,1024,64]{1,2,0:T(8,128)S(1)}, ...), condition=%wide.region_40.40_spmd, body=%wide.region_39.39_spmd.sunk | while | flops 2051212288 | bytes 130318760 | solution.py:169
  2304.1 122.1 %reduce-scatter.11.cloned.1.call-done = bf16[1024,2,2,192]{0,3,2,1:T(8,128)(2,1)} async-done(((bf16[4096,2,2,192]{0,3,2,1:T(8,128)(2,1)}), bf16[1024,2,2,192]{0,3,2,1:T(8,128)(2,1)}) %reduce-scatter.11.cloned.1.call-update) | async-done | bytes 1572880 | tf_op jit(solution)/shard_map/reduce_scatter | solution.py:386
  2433.7 75.6 %all_to_all.58 = bf16[1024,2,3,1,192]{4,1,3,2,0:T(2,128)(2,1)} all-to-all(bf16[1024,2,3,1,192]{4,1,3,2,0:T(2,128)(2,1)} %copy.188), channel_id=1, replica_groups=mesh['fsdp'=2,'ctx'=4,'head'=4] {'head'}, dimensions={0} | all-to-all | bytes 4718592 | tf_op jit(solution)/shard_map/all_to_all | solution.py:395
  2575.9 50.5 %reduce-scatter.13.cloned.1.call-done = bf16[384,2304]{1,0:T(8,128)(2,1)} async-done(((bf16[768,2304]{1,0:T(8,128)(2,1)}), bf16[384,2304]{1,0:T(8,128)(2,1)}) %reduce-scatter.13.cloned.1.call-update) | async-done | bytes 1769488 | tf_op jit(solution)/shard_map/reduce_scatter | solution.py:410
  2698.5 406.7 %all-reduce.13.cloned.1.call-done = (bf16[384,2304]{1,0:T(8,128)(2,1)}, bf16[384,768]{1,0:T(8,128)(2,1)}, bf16[384,4096]{1,0:T(8,128)(2,1)}, bf16[1024,768]{1,0:...) async-done(((bf16[384,2304]{1,0:T(8,128)(2,1)}, bf16[384,768]{1,0:T(8,128)(2,1)}, bf16[384,4096]{1,0:T(8,128)(2,1)}, ...) | async-done | bytes 25952272 | tf_op jit(solution)/shard_map/psum | solution.py:431
  (693 shorter events, 1435.2 us)
Async XLA Ops:
  7.9 181.7 %all-gather.37.cloned.1.call-start = ((), (), s32[]{:S(2)}) async-start(), calls=%async_computation.21 | async-start | bytes 7864320 | tf_op jit(solution)/shard_map/all_gather | solution.py:236
  143.3 158.7 %all-gather.31.cloned.1.call-start = ((), (), s32[]{:S(2)}) async-start(), calls=%async_computation.13 | async-start | bytes 1769472 | tf_op jit(solution)/shard_map/all_gather | solution.py:205
  313.3 144.6 %all-gather.41.cloned.1.call-start = ((), (), s32[]{:S(2)}) async-start(), calls=%async_computation.25 | async-start | bytes 9437184 | tf_op jit(solution)/shard_map/while/body/eval_jaxpr/all_gather | solution.py:291
  317.3 187.6 %all-gather.39.cloned.1.call-start = ((), (), s32[]{:S(2)}) async-start(), calls=%async_computation.24 | async-start | bytes 4718592 | tf_op jit(solution)/shard_map/while/body/eval_jaxpr/all_gather | solution.py:292
  515.4 127.7 %all-gather.39.cloned.1.call-start = ((), (), s32[]{:S(2)}) async-start(), calls=%async_computation.24 | async-start | bytes 4718592 | tf_op jit(solution)/shard_map/while/body/eval_jaxpr/all_gather | solution.py:292
  653.6 127.7 %all-gather.39.cloned.1.call-start = ((), (), s32[]{:S(2)}) async-start(), calls=%async_computation.24 | async-start | bytes 4718592 | tf_op jit(solution)/shard_map/while/body/eval_jaxpr/all_gather | solution.py:292
  791.9 127.7 %all-gather.39.cloned.1.call-start = ((), (), s32[]{:S(2)}) async-start(), calls=%async_computation.24 | async-start | bytes 4718592 | tf_op jit(solution)/shard_map/while/body/eval_jaxpr/all_gather | solution.py:292
  926.8 128.5 %all-gather.35.cloned.1.call-start = ((), (), s32[]{:S(2)}) async-start(), calls=%async_computation.15 | async-start | bytes 4718592 | tf_op jit(solution)/shard_map/all_gather | solution.py:209
  1077.3 169.8 %reduce-scatter.25.cloned.1.call-start = ((), (), s32[]{:S(2)}) async-start(), calls=%async_computation.29 | async-start | bytes 4718592 | tf_op jit(solution)/shard_map/while/body/eval_jaxpr/reduce_scatter | solution.py:349
  1167.4 159.6 %reduce-scatter.23.cloned.1.call-start = ((), (), s32[]{:S(2)}) async-start(), calls=%async_computation.28 | async-start | bytes 9437184 | tf_op jit(solution)/shard_map/while/body/eval_jaxpr/reduce_scatter | solution.py:346
  1334.8 127.1 %all-gather.45.cloned.1.call-start = ((), (), s32[]{:S(2)}) async-start(), calls=%async_computation.27 | async-start | bytes 4718592 | tf_op jit(solution)/shard_map/while/body/eval_jaxpr/all_gather | solution.py:337
  1337.5 169.9 %reduce-scatter.25.cloned.1.call-start = ((), (), s32[]{:S(2)}) async-start(), calls=%async_computation.29 | async-start | bytes 4718592 | tf_op jit(solution)/shard_map/while/body/eval_jaxpr/reduce_scatter | solution.py:349
  1427.6 159.9 %reduce-scatter.23.cloned.1.call-start = ((), (), s32[]{:S(2)}) async-start(), calls=%async_computation.28 | async-start | bytes 9437184 | tf_op jit(solution)/shard_map/while/body/eval_jaxpr/reduce_scatter | solution.py:346
  1595.3 127.1 %all-gather.45.cloned.1.call-start = ((), (), s32[]{:S(2)}) async-start(), calls=%async_computation.27 | async-start | bytes 4718592 | tf_op jit(solution)/shard_map/while/body/eval_jaxpr/all_gather | solution.py:337
  1598.0 170.0 %reduce-scatter.25.cloned.1.call-start = ((), (), s32[]{:S(2)}) async-start(), calls=%async_computation.29 | async-start | bytes 4718592 | tf_op jit(solution)/shard_map/while/body/eval_jaxpr/reduce_scatter | solution.py:349
  1688.0 159.9 %reduce-scatter.23.cloned.1.call-start = ((), (), s32[]{:S(2)}) async-start(), calls=%async_computation.28 | async-start | bytes 9437184 | tf_op jit(solution)/shard_map/while/body/eval_jaxpr/reduce_scatter | solution.py:346
  1858.5 169.9 %reduce-scatter.25.cloned.1.call-start = ((), (), s32[]{:S(2)}) async-start(), calls=%async_computation.29 | async-start | bytes 4718592 | tf_op jit(solution)/shard_map/while/body/eval_jaxpr/reduce_scatter | solution.py:349
  1948.5 159.9 %reduce-scatter.23.cloned.1.call-start = ((), (), s32[]{:S(2)}) async-start(), calls=%async_computation.28 | async-start | bytes 9437184 | tf_op jit(solution)/shard_map/while/body/eval_jaxpr/reduce_scatter | solution.py:346
  2138.8 287.5 %reduce-scatter.11.cloned.1.call-start = ((), (), s32[]{:S(2)}) async-start(), calls=%async_computation.16 | async-start | bytes 7864320 | tf_op jit(solution)/shard_map/reduce_scatter | solution.py:386
  2285.4 262.2 %reduce-scatter.15.cloned.1.call-start = ((), (), s32[]{:S(2)}) async-start(), calls=%async_computation.18 | async-start | bytes 1769472 | tf_op jit(solution)/shard_map/reduce_scatter | solution.py:413
  2288.8 258.9 %reduce-scatter.19.cloned.1.call-start = ((), (), s32[]{:S(2)}) async-start(), calls=%async_computation.20 | async-start | bytes 4718592 | tf_op jit(solution)/shard_map/reduce_scatter | solution.py:425
  2294.2 281.8 %reduce-scatter.17.cloned.1.call-start = ((), (), s32[]{:S(2)}) async-start(), calls=%async_computation.19 | async-start | bytes 9437184 | tf_op jit(solution)/shard_map/reduce_scatter | solution.py:422
  2304.1 322.4 %reduce-scatter.13.cloned.1.call-start = ((), (), s32[]{:S(2)}) async-start(), calls=%async_computation.17 | async-start | bytes 5308416 | tf_op jit(solution)/shard_map/reduce_scatter | solution.py:410
  2547.5 557.7 %all-reduce.13.cloned.1.call-start = ((), (), s32[]{:S(2)}) async-start(), calls=%async_computation.23 | async-start | bytes 51904512 | tf_op jit(solution)/shard_map/psum | solution.py:431
  (138 other events, 4132.6 us)
Sparse Core Ops, SparseCore 0:
  9.6 51.3 all-gather.28
  143.4 46.1 all-gather.36
  317.4 140.4 all-gather.40
  459.9 44.9 all-gather.38
  515.5 80.3 all-gather.40
  598.1 44.9 all-gather.38
  653.8 80.3 all-gather.40
  736.4 44.9 all-gather.38
  792.0 80.3 all-gather.40
  874.6 44.9 all-gather.38
  928.3 80.4 all-gather.32
  1074.7 80.3 all-gather.42
  1249.9 77.0 reduce-scatter.22
  1334.9 80.3 all-gather.42
  1416.9 44.9 all-gather.44
  1510.3 77.0 reduce-scatter.22
  1595.4 80.3 all-gather.42
  1770.8 77.0 reduce-scatter.22
  1855.9 80.3 all-gather.42
  2031.3 77.0 reduce-scatter.22
  2285.5 140.7 reduce-scatter.10
  2498.8 77.0 reduce-scatter.16
  2578.8 47.6 reduce-scatter.12
  2647.2 458.0 all-reduce.12
  (12 shorter events, 450.7 us)
where the time goes:
time: 3150 us; the launch traced here: 3140 us
  waiting for transfers between devices  2150 us (68%)
  matrix products  340 us (11%)
  local copies, waits for them, and re-layouts  270 us (9%)
  blocking collectives  189 us (6%)
  other arithmetic  161 us (5%)
    psum x1, waiting for transfers between devices, on_device(): lax.psum(dense_shares[1].astype(jnp.bfloat16), ('ctx', 'head'))  407 us
    all_gather x4, waiting for transfers between devices, expert_forward(): lax.all_gather(local_in, 'fsdp', axis=0, tiled=True)  371 us
    all_gather x4, waiting for transfers between devices, expert_backward(): lax.all_gather(local_in, 'fsdp', axis=0, tiled=True)  311 us
    reduce_scatter x4, waiting for transfers between devices, expert_backward(): lax.psum_scatter(in_grad.astype(jnp.bfloat16), 'fsdp', scatter_dimension=...  309 us
    all_gather x4, waiting for transfers between devices, expert_forward(): lax.all_gather(local_out, 'fsdp', axis=0, tiled=True)  159 us
    all_gather x4, waiting for transfers between devices, expert_backward(): lax.all_gather(local_out, 'fsdp', axis=0, tiled=True)  137 us
    reduce_scatter x1, waiting for transfers between devices, on_device(): lax.psum_scatter(key_terms.astype(jnp.bfloat16), 'ctx', scatter_dimension...  122 us
    reduce_scatter x4, waiting for transfers between devices, expert_backward(): lax.psum_scatter(out_grad.astype(jnp.bfloat16), 'fsdp', scatter_dimension...  92.3 us
  transfers between devices with their start and end apart: 38, of which 34 were waited for; matrix products, arithmetic and copies ran while one was open for 14% of the time, Pallas kernels for 0%

commit v1 on v0

v1 whole, which is shorter than its diff:
```python
import functools
import math

import jax
import jax.numpy as jnp
from jax import lax
from jax.experimental import pallas as pl
from jax.experimental.pallas import tpu as pltpu
from jax.sharding import PartitionSpec as P

HEAD_DIM = 64
EPS = 1e-06
NEG = -1e30
ROPE_BASE = 10000.0
BF = jnp.bfloat16
F32 = jnp.float32
MB = 1 << 20


def swap_with(value, axis_name, bit):
    size = lax.axis_size(axis_name)
    return lax.ppermute(value, axis_name, [(i, i ^ bit) for i in range(size)])


def fsdp_gather(value, axis):
    return lax.all_gather(value, "fsdp", axis=axis, tiled=True)


def fsdp_scatter(value, axis):
    count = lax.axis_size("fsdp")
    if count != 2:
        return lax.psum_scatter(value, "fsdp", scatter_dimension=axis, tiled=True)
    mine = lax.axis_index("fsdp")
    part = value.shape[axis] // 2
    sent = lax.dynamic_slice_in_dim(value, (1 - mine) * part, part, axis)
    kept = lax.dynamic_slice_in_dim(value, mine * part, part, axis)
    got = swap_with(sent, "fsdp", 1)
    return (kept.astype(F32) + got.astype(F32)).astype(value.dtype)


def line_gather(value, axis):
    count = lax.axis_size("head")
    mine = lax.axis_index("head")
    part = value.shape[axis]
    up = [(i, i + 1) for i in range(count - 1)]
    down = [(i + 1, i) for i in range(count - 1)]
    below, above = [], []
    rising, falling = value, value
    for _ in range(count - 1):
        rising = lax.ppermute(rising, "head", up)
        falling = lax.ppermute(falling, "head", down)
        below.insert(0, rising)
        above.append(falling)
    line = jnp.concatenate(below + [value] + above, axis=axis)
    return lax.dynamic_slice_in_dim(line, (count - 1 - mine) * part, count * part, axis)


def line_scatter(value, axis):
    count = lax.axis_size("head")
    mine = lax.axis_index("head")
    part = value.shape[axis] // count
    up = [(i, i + 1) for i in range(count - 1)]
    down = [(i + 1, i) for i in range(count - 1)]

    def block(index):
        index = jnp.clip(index, 0, count - 1)
        return lax.dynamic_slice_in_dim(value, index * part, part, axis).astype(F32)

    rising, falling = None, None
    for step in range(count - 1):
        upward = block(count - 1 - step + mine)
        downward = block(step - (count - 1) + mine)
        if step:
            upward = upward + rising.astype(F32)
            downward = downward + falling.astype(F32)
        rising = lax.ppermute(upward.astype(BF), "head", up)
        falling = lax.ppermute(downward.astype(BF), "head", down)
    return block(mine) + rising.astype(F32) + falling.astype(F32)


def ctx_gather(value):
    blocks = [value]
    bit = lax.axis_size("ctx") // 2
    found = {0: value}
    while bit:
        for k in list(found):
            found[k ^ bit] = swap_with(found[k], "ctx", bit)
        bit //= 2
    blocks = [found[k] for k in range(len(found))]
    return blocks


def ctx_scatter(blocks):
    held = {k: blocks[k] for k in range(len(blocks))}
    bit = 1
    while len(held) > 1:
        kept = {}
        for k in list(held):
            if not k & bit:
                got = swap_with(held[k | bit], "ctx", bit)
                kept[k] = held[k].astype(F32) + got.astype(F32)
        held = {k: (v if len(kept) == 1 else v.astype(BF)) for k, v in kept.items()}
        bit *= 2
    return held[0]


def dot_t(a, b):
    return lax.dot_general(a, b, (((1,), (1,)), ((), ())), preferred_element_type=F32)


def dot_l(a, b):
    return lax.dot_general(a, b, (((0,), (0,)), ((), ())), preferred_element_type=F32)


def dot(a, b):
    return jnp.dot(a, b, preferred_element_type=F32)


def attend_forward(ctx, bounds, queries, keys_values, starts):
    seqs, rows, width = queries.shape
    heads = width // HEAD_DIM
    blocks = keys_values.shape[0]
    tq, tk = min(256, rows), min(512, rows)
    per = rows // tk

    def kernel(ctx_ref, bounds_ref, q_ref, kv_ref, seg_ref, o_ref, low_ref, lse_ref):
        s, i = pl.program_id(0), pl.program_id(1)
        here = ctx_ref[0]
        seg = seg_ref[0]
        row_pos = here * rows + i * tq + lax.broadcasted_iota(jnp.int32, (tq, tk), 0)
        lane = lax.broadcasted_iota(jnp.int32, (tq, tk), 1)

        def step(masked, t, carry):
            at = lax.div(t, per) ^ here
            off = pl.multiple_of(lax.rem(t, per) * tk, tk)
            new = []
            if masked:
                key_pos = t * tk + lane
                seen = (key_pos <= row_pos) & (key_pos >= seg)
            for h in range(heads):
                top, total, acc = carry[3 * h : 3 * h + 3]
                cols = slice(h * HEAD_DIM, (h + 1) * HEAD_DIM)
                vals = slice(width + h * HEAD_DIM, width + (h + 1) * HEAD_DIM)
                scores = dot_t(q_ref[0, :, cols], kv_ref[at, 0, pl.ds(off, tk), cols])
                if masked:
                    scores = jnp.where(seen, scores, NEG)
                new_top = jnp.maximum(top, jnp.max(scores, axis=1, keepdims=True))
                weights = jnp.exp(scores - new_top)
                fade = jnp.exp(top - new_top)
                total = total * fade + jnp.sum(weights, axis=1, keepdims=True)
                acc = acc * fade + dot(weights.astype(BF), kv_ref[at, 0, pl.ds(off, tk), vals])
                new += [new_top, total, acc]
            return tuple(new)

        carry = (
            jnp.full((tq, 1), NEG, F32),
            jnp.zeros((tq, 1), F32),
            jnp.zeros((tq, HEAD_DIM), F32),
        ) * heads
        b = [bounds_ref[s, i, n] for n in range(4)]
        carry = lax.fori_loop(b[0], b[1], functools.partial(step, True), carry)
        carry = lax.fori_loop(b[1], b[2], functools.partial(step, False), carry)
        carry = lax.fori_loop(b[2], b[3], functools.partial(step, True), carry)
        column = lax.broadcasted_iota(jnp.int32, (tq, 128), 1)
        lse = jnp.zeros((tq, 128), F32)
        outs = []
        for h in range(heads):
            top, total, acc = carry[3 * h : 3 * h + 3]
            outs.append(acc / total)
            lse = jnp.where(column == h, top + jnp.log(total), lse)
        result = jnp.concatenate(outs, axis=1)
        o_ref[0] = result
        low_ref[0] = result.astype(BF)
        lse_ref[0] = lse

    return pl.pallas_call(
        kernel,
        out_shape=(
            jax.ShapeDtypeStruct((seqs, rows, width), F32),
            jax.ShapeDtypeStruct((seqs, rows, width), BF),
            jax.ShapeDtypeStruct((seqs, rows, 128), F32),
        ),
        grid_spec=pltpu.PrefetchScalarGridSpec(
            num_scalar_prefetch=2,
            grid=(seqs, rows // tq),
            in_specs=[
                pl.BlockSpec((1, tq, width), lambda s, i, *_: (s, i, 0)),
                pl.BlockSpec((blocks, 1, rows, 2 * width), lambda s, i, *_: (0, s, 0, 0)),
                pl.BlockSpec((1, tq, 1), lambda s, i, *_: (s, i, 0)),
            ],
            out_specs=[
                pl.BlockSpec((1, tq, width), lambda s, i, *_: (s, i, 0)),
                pl.BlockSpec((1, tq, width), lambda s, i, *_: (s, i, 0)),
                pl.BlockSpec((1, tq, 128), lambda s, i, *_: (s, i, 0)),
            ],
        ),
        compiler_params=pltpu.CompilerParams(vmem_limit_bytes=48 * MB),
        name="attend_forward",
        cost_estimate=pl.CostEstimate(
            flops=int(2 * 2 * seqs * heads * rows * rows * 3.5 * HEAD_DIM * 4),
            bytes_accessed=16 * MB,
            transcendentals=int(seqs * heads * rows * rows * 3.5),
        ),
    )(ctx, bounds, queries, keys_values, starts)


def attend_backward(ctx, bounds, edges, queries, keys_values, grads, stats, starts):
    seqs, rows, width = queries.shape
    heads = width // HEAD_DIM
    blocks = keys_values.shape[0]
    tq, tk = min(512, rows), min(512, rows)
    per = rows // tk

    def kernel(ctx_ref, bounds_ref, edges_ref, q_ref, kv_ref, do_ref, stat_ref, seg_ref, dq_ref, dkv_ref, acc):
        s, t = pl.program_id(0), pl.program_id(1)
        here = ctx_ref[0]

        @pl.when(t == 0)
        def _():
            dq_ref[...] = jnp.zeros_like(dq_ref)

        acc[...] = jnp.zeros_like(acc)
        lane = lax.broadcasted_iota(jnp.int32, (tk, tq), 1)
        key_pos = t * tk + lax.broadcasted_iota(jnp.int32, (tk, tq), 0)

        def tile(masked, i):
            off = pl.multiple_of(i * tq, tq)
            if masked:
                row_pos = here * rows + off + lane
                seen = (key_pos <= row_pos) & (key_pos >= seg_ref[0, 0:1, pl.ds(off, tq)])
            for h in range(heads):
                cols = slice(h * HEAD_DIM, (h + 1) * HEAD_DIM)
                vals = slice(width + h * HEAD_DIM, width + (h + 1) * HEAD_DIM)
                q = q_ref[0, pl.ds(off, tq), cols]
                do = do_ref[0, pl.ds(off, tq), cols]
                k = kv_ref[0, 0, :, cols]
                v = kv_ref[0, 0, :, vals]
                scores = dot_t(k, q)
                weights = jnp.exp(scores - stat_ref[0, h : h + 1, pl.ds(off, tq)])
                if masked:
                    weights = jnp.where(seen, weights, 0.0)
                dweights = dot_t(v, do)
                dscores = weights * (dweights - stat_ref[0, heads + h : heads + h + 1, pl.ds(off, tq)])
                dscores = dscores.astype(BF)
                acc[h] += dot(dscores, q)
                acc[heads + h] += dot(weights.astype(BF), do)
                dq_ref[0, pl.ds(off, tq), cols] += dot_l(dscores, k)

        def step(i, carry):
            first = here * rows + i * tq
            clear = (edges_ref[s, i] <= t * tk) & (t * tk + tk - 1 <= first)

            @pl.when(clear)
            def _():
                tile(False, i)

            @pl.when(jnp.logical_not(clear))
            def _():
                tile(True, i)

            return carry

        lax.fori_loop(bounds_ref[s, t, 0], bounds_ref[s, t, 1], step, 0)
        dkv_ref[0, 0] = jnp.concatenate([acc[n] for n in range(2 * heads)], axis=1).astype(BF)

    return pl.pallas_call(
        kernel,
        out_shape=(
            jax.ShapeDtypeStruct((seqs, rows, width), F32),
            jax.ShapeDtypeStruct((blocks, seqs, rows, 2 * width), BF),
        ),
        grid_spec=pltpu.PrefetchScalarGridSpec(
            num_scalar_prefetch=3,
            grid=(seqs, blocks * per),
            in_specs=[
                pl.BlockSpec((1, rows, width), lambda s, t, *_: (s, 0, 0)),
                pl.BlockSpec((1, 1, tk, 2 * width), lambda s, t, c, *_: ((t // per) ^ c[0], s, t % per, 0)),
                pl.BlockSpec((1, rows, width), lambda s, t, *_: (s, 0, 0)),
                pl.BlockSpec((1, 8, rows), lambda s, t, *_: (s, 0, 0)),
                pl.BlockSpec((1, 1, rows), lambda s, t, *_: (s, 0, 0)),
            ],
            out_specs=[
                pl.BlockSpec((1, rows, width), lambda s, t, *_: (s, 0, 0)),
                pl.BlockSpec((1, 1, tk, 2 * width), lambda s, t, c, *_: ((t // per) ^ c[0], s, t % per, 0)),
            ],
            scratch_shapes=[pltpu.VMEM((2 * heads, tk, HEAD_DIM), F32)],
        ),
        compiler_params=pltpu.CompilerParams(vmem_limit_bytes=48 * MB),
        name="attend_backward",
        cost_estimate=pl.CostEstimate(
            flops=int(5 * 2 * seqs * heads * rows * rows * 3.5 * HEAD_DIM * 4),
            bytes_accessed=32 * MB,
            transcendentals=int(seqs * heads * rows * rows * 3.5),
        ),
    )(ctx, bounds, edges, queries, keys_values, grads, stats, starts)


def gated_mlp(rows_in, rows_in_t, grads, grads_t, gates, w_in, w_out, y_before, dx_before):
    count, width = rows_in.shape
    hidden = w_out.shape[0]
    tile = min(256, hidden)
    chunk = min(512, count)
    steps = hidden // tile
    first = y_before is None

    def kernel(*refs):
        x_ref, xt_ref, d_ref, dt_ref, c_ref, wg_ref, wu_ref, wo_ref = refs[:8]
        refs = refs[8:]
        if not first:
            yb_ref, dxb_ref = refs[:2]
            refs = refs[2:]
        y_ref, dx_ref, dc_ref, din_ref, dout_ref, a_s, g_s, u_s = refs
        j = pl.program_id(0)

        @pl.when(j == 0)
        def _():
            dc_ref[...] = jnp.zeros_like(dc_ref)
            if first:
                y_ref[...] = jnp.zeros_like(y_ref)
                dx_ref[...] = jnp.zeros_like(dx_ref)
            else:
                y_ref[...] = yb_ref[...]
                dx_ref[...] = dxb_ref[...]

        def body(n, carry):
            at = pl.ds(pl.multiple_of(n * chunk, chunk), chunk)
            x = x_ref[at, :]
            gate = dot(x, wg_ref[...])
            up = dot(x, wu_ref[...])
            raw = dot_t(d_ref[at, :], wo_ref[...])
            c = c_ref[at, :]
            sig = 1.0 / (1.0 + jnp.exp(-gate))
            silu = gate * sig
            act = silu * up
            dc_ref[at, :] += jnp.sum(act * raw, axis=1, keepdims=True)
            back = raw * c
            a_low = (act * c).astype(BF)
            dg = (back * up * (sig + silu * (1.0 - sig))).astype(BF)
            du = (back * silu).astype(BF)
            a_s[at, :] = a_low
            g_s[at, :] = dg
            u_s[at, :] = du
            y_ref[at, :] += dot(a_low, wo_ref[...])
            dx_ref[at, :] += dot_t(dg, wg_ref[...]) + dot_t(du, wu_ref[...])
            return carry

        lax.fori_loop(0, count // chunk, body, 0)
        part = min(256, width)

        def weights(n, carry):
            at = pl.ds(pl.multiple_of(n * part, part), part)
            xt = xt_ref[at, :]
            din_ref[0, at, :] = dot(xt, g_s[...]).astype(BF)
            din_ref[1, at, :] = dot(xt, u_s[...]).astype(BF)
            return carry

        lax.fori_loop(0, width // part, weights, 0)
        for n in range(width // part):
            dout_ref[:, n * part : (n + 1) * part] = dot(dt_ref[n * part : (n + 1) * part, :], a_s[...]).T.astype(BF)

    once = pl.Buffered(1)
    whole = lambda *shape: pl.BlockSpec(shape, lambda j: (0,) * len(shape), pipeline_mode=once)
    in_specs = [
        whole(count, width),
        whole(width, count),
        whole(count, width),
        whole(width, count),
        whole(count, 1),
        pl.BlockSpec((width, tile), lambda j: (0, j)),
        pl.BlockSpec((width, tile), lambda j: (0, j + steps)),
        pl.BlockSpec((tile, width), lambda j: (j, 0)),
    ]
    operands = [rows_in, rows_in_t, grads, grads_t, gates, w_in, w_in, w_out]
    if not first:
        in_specs += [whole(count, width), whole(count, width)]
        operands += [y_before, dx_before]
    return pl.pallas_call(
        kernel,
        out_shape=(
            jax.ShapeDtypeStruct((count, width), F32),
            jax.ShapeDtypeStruct((count, width), F32),
            jax.ShapeDtypeStruct((count, 1), F32),
            jax.ShapeDtypeStruct((2, width, hidden), BF),
            jax.ShapeDtypeStruct((hidden, width), BF),
        ),
        grid=(steps,),
        in_specs=in_specs,
        out_specs=[
            whole(count, width),
            whole(count, width),
            whole(count, 1),
            pl.BlockSpec((2, width, tile), lambda j: (0, 0, j)),
            pl.BlockSpec((tile, width), lambda j: (j, 0)),
        ],
        scratch_shapes=[pltpu.VMEM((count, tile), BF)] * 3,
        compiler_params=pltpu.CompilerParams(vmem_limit_bytes=60 * MB),
        name="gated_mlp",
        cost_estimate=pl.CostEstimate(
            flops=9 * 2 * count * width * hidden,
            bytes_accessed=40 * MB,
            transcendentals=count * hidden,
        ),
    )(*operands)


def inverse_rms(values):
    return lax.rsqrt(jnp.mean(values * values, axis=-1, keepdims=True) + EPS)


def norm_back(values, inverse, gain, grad):
    scaled = grad * gain
    dotted = jnp.mean(scaled * values, axis=-1, keepdims=True)
    return inverse * scaled - values * (inverse * inverse * inverse) * dotted


def swap_halves(weight, heads):
    rows = weight.shape[0]
    pairs = weight.reshape(rows, heads, 2, HEAD_DIM // 2)
    return pairs[:, :, ::-1].reshape(rows, heads * HEAD_DIM)


def on_device(
    tokens,
    segment_ids,
    routes,
    cotangent,
    norm1_gain,
    qkv_weight,
    out_weight,
    norm2_gain,
    router_weight,
    shared_in,
    shared_out,
    expert_in,
    expert_out,
):
    local_len, seqs, width = tokens.shape
    count = local_len * seqs
    groups = lax.axis_size("head")
    ctxs = lax.axis_size("ctx")
    shards = lax.axis_size("fsdp")
    ctx = lax.axis_index("ctx")
    head = lax.axis_index("head")
    shard = lax.axis_index("fsdp")
    group_width = width // groups
    heads = group_width // HEAD_DIM
    block = local_len * groups
    span = seqs * block
    experts = expert_in.shape[0]
    ff = expert_in.shape[2] // 2
    fs = shared_in.shape[1] // 2
    fs_part = fs // ctxs
    ctx_word = ctx.astype(jnp.int32).reshape(1)

    x_own = tokens.transpose(1, 0, 2)
    x_line = line_gather(x_own, 1)
    small = jnp.concatenate([norm1_gain[None], norm2_gain[None], router_weight.T], axis=0)
    small = fsdp_gather(small, 1)
    gain_one, gain_two = small[0].astype(F32), small[1].astype(F32)
    w_router = small[2:]
    w_group = lax.dynamic_index_in_dim(qkv_weight.reshape(-1, 3, groups, group_width), head, 2, keepdims=False)
    w_group = fsdp_gather(w_group.reshape(-1, 3 * group_width), 0)
    w_rot = w_group[:, : 2 * group_width]
    w_all = jnp.concatenate([w_rot, swap_halves(w_rot, 2 * heads), w_group[:, 2 * group_width :]], axis=1)

    dz_own = cotangent.transpose(1, 0, 2).reshape(count, width)
    dz_all = jnp.concatenate(ctx_gather(dz_own), axis=0)
    w_attn = fsdp_gather(out_weight, 0)
    w_expert_in = fsdp_gather(lax.dynamic_index_in_dim(expert_in, ctx, 0, keepdims=False), 0)
    w_expert_out = fsdp_gather(lax.dynamic_index_in_dim(expert_out, ctx, 0, keepdims=False), 0)
    piece = fs // shards // ctxs
    s_in = shared_in.reshape(-1, 2, shards, ctxs, piece)
    s_in = lax.dynamic_index_in_dim(s_in, ctx, 3, keepdims=False).reshape(-1, 2 * fs_part)
    w_shared_in = fsdp_gather(s_in, 0)
    w_shared_out = fsdp_gather(lax.dynamic_slice_in_dim(shared_out, ctx * piece, piece, 0), 0)

    index = jnp.arange(HEAD_DIM // 2).astype(F32)
    freq = jnp.exp(-math.log(ROPE_BASE) * 2.0 * index / HEAD_DIM)
    position = ctx * block + jnp.arange(block, dtype=jnp.int32)
    angle = position.astype(F32)[:, None] * freq[None, :]
    cosine, sine = jnp.cos(angle), jnp.sin(angle)
    cos_all = jnp.tile(cosine, (1, 4 * heads))[None]
    sin_all = jnp.tile(jnp.concatenate([-sine, sine], axis=1), (1, 2 * heads))[None]

    x_f = x_line.astype(F32)
    inverse_one = inverse_rms(x_f)
    normed = (x_f * inverse_one * gain_one).astype(BF)
    mixed = dot(normed.reshape(span, width), w_all).reshape(seqs, block, 5 * group_width)
    rot = 2 * group_width
    rotated = mixed[:, :, :rot] * cos_all + mixed[:, :, rot : 2 * rot] * sin_all
    queries = rotated[:, :, :group_width].astype(BF) * jnp.asarray(HEAD_DIM**-0.5, BF)
    key_value = jnp.concatenate([rotated[:, :, group_width:], mixed[:, :, 2 * rot :]], axis=2).astype(BF)
    kv_all = jnp.stack(ctx_gather(key_value))

    def forward_bounds(tq, tk):
        nq = block // tq
        first = ctx * block + jnp.arange(nq, dtype=jnp.int32) * tq
        low = segment_ids[:, ::tq] // tk
        last_start = segment_ids[:, tq - 1 :: tq]
        clear_to = jnp.broadcast_to(first // tk, low.shape)
        clear_from = jnp.minimum((last_start + tk - 1) // tk, clear_to)
        clear_from = jnp.maximum(clear_from, low)
        clear_to = jnp.maximum(clear_to, clear_from)
        high = jnp.broadcast_to((first + tq - 1) // tk + 1, low.shape)
        return jnp.stack([low, clear_from, clear_to, high], axis=2).astype(jnp.int32)

    attended, attended_low, lse = attend_forward(
        ctx_word,
        forward_bounds(min(256, block), min(512, block)),
        queries,
        kv_all,
        segment_ids[:, :, None],
    )
    sent = attended_low.reshape(seqs, groups, local_len, group_width)
    back = lax.all_to_all(sent, "head", split_axis=1, concat_axis=3, tiled=True)
    attn_rows = back.reshape(count, width)

    x_rows = x_own.reshape(count, width).astype(F32)
    hidden = x_rows + dot(attn_rows, w_attn)
    inverse_two = inverse_rms(hidden)
    normed_two = (hidden * inverse_two * gain_two).astype(BF)
    route_rows = routes.reshape(local_len, seqs, 2).transpose(1, 0, 2).reshape(count, 2)
    logits = dot_t(normed_two, w_router)
    ids = jnp.arange(experts, dtype=jnp.int32)
    picks = (route_rows[:, :, None] == ids).astype(F32)
    chosen = jnp.sum(logits[:, None, :] * picks, axis=2)
    gate_first = 1.0 / (1.0 + jnp.exp(chosen[:, 1:] - chosen[:, :1]))
    gates = jnp.concatenate([gate_first, 1.0 - gate_first], axis=1)
    combine = jnp.sum(gates[:, :, None] * picks, axis=1)

    xn_all = jnp.concatenate(ctx_gather(normed_two), axis=0)
    combine_all = jnp.concatenate(ctx_gather(combine.T), axis=1)
    c_own = lax.dynamic_index_in_dim(combine_all, ctx, 0, keepdims=False)[:, None]
    xn_t = xn_all.T
    dz_t = dz_all.T
    y_part, dx_part, dc, ge_in, ge_out = gated_mlp(
        xn_all, xn_t, dz_all, dz_t, c_own, w_expert_in, w_expert_out, None, None
    )
    y_part, dx_part, _, gs_in, gs_out = gated_mlp(
        xn_all, xn_t, dz_all, dz_t, jnp.ones_like(c_own), w_shared_in, w_shared_out, y_part, dx_part
    )
    dc_blocks = dc.reshape(ctxs, count)
    dc_got = [dc_blocks[0]] + [
        lax.ppermute(dc_blocks[k], "ctx", [(i, i ^ k) for i in range(ctxs)]) for k in range(1, ctxs)
    ]
    dcombine = sum(
        dc_got[k][:, None] * ((ctx ^ k) == ids).astype(F32)[None, :] for k in range(ctxs)
    )
    dx_low = dx_part.astype(BF).reshape(ctxs, count, width)
    dxn2 = ctx_scatter([dx_low[k] for k in range(ctxs)])
    y_low = y_part.astype(BF).reshape(ctxs, count, width)
    y_own = ctx_scatter([y_low[k] for k in range(ctxs)])
    output = (hidden + y_own).astype(BF).reshape(seqs, local_len, width).transpose(1, 0, 2)

    dchosen = jnp.sum(dcombine[:, None, :] * picks, axis=2)
    dfirst = gates[:, :1] * gates[:, 1:] * (dchosen[:, :1] - dchosen[:, 1:])
    dlogits = (dfirst * (picks[:, 0] - picks[:, 1])).astype(BF)
    router_grad = dot_l(dlogits, normed_two)
    dxn2 = dxn2 + dot(dlogits, w_router)
    dz_rows = dz_own.astype(F32)
    dh = dz_rows + norm_back(hidden, inverse_two, gain_two, dxn2)
    gain_two_grad = jnp.sum(dxn2 * hidden * inverse_two, axis=0)
    dh_low = dh.astype(BF)
    g_attn = dot_l(attn_rows, dh_low).astype(BF)
    dattn = dot_t(dh_low, w_attn).astype(BF).reshape(seqs, local_len, width)
    grad_out = lax.all_to_all(
        dattn.reshape(seqs, local_len, groups, group_width), "head", split_axis=2, concat_axis=1, tiled=True
    ).reshape(seqs, block, group_width)

    delta = jnp.sum((grad_out.astype(F32) * attended).reshape(seqs, block, heads, HEAD_DIM), axis=3)
    stats = jnp.concatenate(
        [lse[:, :, :heads].transpose(0, 2, 1), delta.transpose(0, 2, 1), jnp.zeros((seqs, 8 - 2 * heads, block), F32)],
        axis=1,
    )
    tq = tk = min(512, block)
    tile_last = ctx * block + (jnp.arange(block // tq, dtype=jnp.int32) + 1) * tq - 1
    tile_key = jnp.arange(ctxs * block // tk, dtype=jnp.int32)
    q_low = jnp.sum((tile_last[None, :] < (tile_key * tk)[:, None]).astype(jnp.int32), axis=1)
    q_high = jnp.sum(((segment_ids[:, ::tq] // tk)[:, None, :] <= tile_key[None, :, None]).astype(jnp.int32), axis=2)
    q_low = jnp.broadcast_to(q_low, q_high.shape)
    back_bounds = jnp.stack([q_low, q_high], axis=2).astype(jnp.int32)
    dq, dkv_parts = attend_backward(
        ctx_word,
        back_bounds,
        segment_ids[:, tq - 1 :: tq],
        queries,
        kv_all,
        grad_out,
        stats,
        segment_ids[:, None, :],
    )
    dkv = ctx_scatter([dkv_parts[k] for k in range(ctxs)])
    dq = dq * (HEAD_DIM**-0.5)
    d_rot = jnp.concatenate([dq, dkv[:, :, :group_width]], axis=2).astype(BF).astype(F32)
    d_all = jnp.concatenate(
        [d_rot * cos_all, d_rot * sin_all, dkv[:, :, group_width:]], axis=2
    ).astype(BF).reshape(span, 5 * group_width)
    dxn1_part = dot_t(d_all, w_all).reshape(seqs, block, width)
    g_all = dot_l(normed.reshape(span, width), d_all)
    g_rot = g_all[:, :rot] + swap_halves(g_all[:, rot : 2 * rot], 2 * heads)
    g_qkv = jnp.concatenate([g_rot, g_all[:, 2 * rot :]], axis=1).astype(BF)
    gain_one_grad = jnp.sum(dxn1_part * x_f * inverse_one, axis=(0, 1))
    dxn1 = line_scatter(dxn1_part.astype(BF), 1).reshape(count, width)
    dx_norm = norm_back(x_rows, inverse_rms(x_rows), gain_one, dxn1)
    tokens_grad = (dh + dx_norm).reshape(seqs, local_len, width).transpose(1, 0, 2)

    def share(grad, axis, split):
        part = fsdp_scatter(grad, axis)
        part = line_scatter(part, split).astype(BF)
        return line_gather(part, split)

    def place(blocks, shape):
        out = jnp.zeros((ctxs,) + shape, F32)
        for k, blk in enumerate(blocks):
            out = lax.dynamic_update_slice_in_dim(out, blk.astype(F32).reshape((1,) + shape), ctx ^ k, 0)
        return out

    ge_in = ctx_gather(share(ge_in, 1, 1))
    ge_out = ctx_gather(share(ge_out, 0, 0))
    gs_in = ctx_gather(share(gs_in, 1, 1))
    gs_out = ctx_gather(share(gs_out, 0, 0))
    rows_per = width // shards
    expert_in_grad = place([g.transpose(1, 0, 2) for g in ge_in], (rows_per, 2 * ff))
    expert_out_grad = place(ge_out, (ff // shards, width))
    shared_in_grad = place(gs_in, (2, rows_per, shards, piece)).transpose(2, 1, 3, 0, 4).reshape(rows_per, 2 * fs)
    shared_out_grad = place(gs_out, (piece, width)).reshape(fs // shards, width)

    g_qkv = fsdp_scatter(g_qkv, 0)
    g_qkv = lax.psum(g_qkv, "ctx")
    g_qkv = line_gather(g_qkv[:, None], 1).astype(F32)
    qkv_grad = g_qkv.reshape(rows_per, groups, 3, group_width).transpose(0, 2, 1, 3).reshape(rows_per, 3 * width)
    g_attn = fsdp_scatter(g_attn, 0)
    out_grad = lax.psum(g_attn, ("ctx", "head")).astype(F32)
    tiny = jnp.concatenate([gain_one_grad[None], gain_two_grad[None], router_grad], axis=0)
    tiny = lax.psum(tiny, ("fsdp", "ctx", "head"))
    tiny = lax.dynamic_slice_in_dim(tiny, shard * rows_per, rows_per, 1)
    return (
        output,
        tokens_grad,
        tiny[0],
        qkv_grad,
        out_grad,
        tiny[1],
        tiny[2:].T,
        shared_in_grad,
        shared_out_grad,
        expert_in_grad,
        expert_out_grad,
    )


def solution(mesh):
    rows = P(("ctx", "head"), "fsdp", None)
    vector = P("fsdp")
    matrix = P("fsdp", None)
    stack = P(None, "fsdp", None)
    return jax.shard_map(
        on_device,
        mesh=mesh,
        in_specs=(
            rows,
            P("fsdp", "ctx"),
            P(("ctx", "head"), "fsdp", None, None),
            rows,
            vector,
            matrix,
            matrix,
            vector,
            matrix,
            matrix,
            matrix,
            stack,
            stack,
        ),
        out_specs=(rows, rows, vector, matrix, matrix, vector, matrix, matrix, matrix, stack, stack),
        check_vma=False,
    )
```

time: 3150 us -> 1350 us (0.43)
  waiting for transfers between devices: 2150 us -> 196 us
  matrix products: 340 us -> 22.1 us
  starting transfers between devices: 10.1 us -> 310 us
  Pallas kernels: 0 us -> 191 us
  local copies, waits for them, and re-layouts: 270 us -> 422 us
  blocking collectives: 189 us -> 74.9 us
  other arithmetic: 161 us -> 110 us
    all_gather x21 -> x4, waiting for transfers between devices: 1120 us -> 0.03 us  [fsdp_gather(): return lax.all_gather(value, 'fsdp', axis=axis, tiled=True)]
    reduce_scatter x13 -> x0, waiting for transfers between devices: 602 us -> none  [the longest x4 309 us: expert_backward(): lax.psum_scatter(in_grad.astype(jnp.bfloat16), 'fsdp', scatter_dimension=...]
    psum x1 -> x2, waiting for transfers between devices: 407 us -> 31.5 us  [the longest x1 20.3 us: on_device(): g_qkv = lax.psum(g_qkv, 'ctx')]
    dot_general x71 -> x9, matrix products: 340 us -> 22.1 us  [the longest x3 8.21 us: dot_t(): lax.dot_general(a, b, (((1,), (1,)), ((), ())), preferred_element_type=F32)]
    ppermute x0 -> x108, starting transfers between devices: none -> 303 us  [the longest x39 116 us: swap_with(): return lax.ppermute(value, axis_name, [(i, i ^ bit) for i in range(size)])]
    pallas_call x0 -> x4, Pallas kernels: none -> 191 us  [the longest x2 117 us: gated_mlp(): pl.pallas_call(kernel, out_shape=(jax.ShapeDtypeStruct((count, width), F3...]
    ppermute x0 -> x108, waiting for transfers between devices: none -> 164 us  [the longest x18 52.7 us: line_gather(): falling = lax.ppermute(falling, 'head', down)]
    dynamic_update_slice x6 -> x8, local copies, waits for them, and re-layouts: 9.63 us -> 153 us  [place(): lax.dynamic_update_slice_in_dim(out, blk.astype(F32).reshape((1,) + shape...]
  transfers between devices with their start and end apart: 38 -> 116, of which waited for: 34 -> 28; matrix products, arithmetic and copies ran while one was open for 14% -> 39% of each run, Pallas kernels for 0% -> 14%
where the time goes in v1:
time: 1350 us; the launch traced here: 1340 us
  local copies, waits for them, and re-layouts  422 us (31%)
  starting transfers between devices  310 us (23%)
  waiting for transfers between devices  196 us (15%)
  Pallas kernels  191 us (14%)
  other arithmetic  110 us (8%)
  blocking collectives  74.9 us (6%)
  matrix products  22.1 us (2%)
  between operations  16.8 us (1%)
    dynamic_update_slice x8, local copies, waits for them, and re-layouts, place(): lax.dynamic_update_slice_in_dim(out, blk.astype(F32).reshape((1,) + shape...  153 us
    pallas_call x2, Pallas kernels, gated_mlp(): pl.pallas_call(kernel, out_shape=(jax.ShapeDtypeStruct((count, width), F3...  117 us
    ppermute x39, starting transfers between devices, swap_with(): return lax.ppermute(value, axis_name, [(i, i ^ bit) for i in range(size)])  116 us
    ppermute x18, starting transfers between devices, line_gather(): rising = lax.ppermute(rising, 'head', up)  74.9 us
    reshape x16, local copies, waits for them, and re-layouts, place(): blk.astype(F32).reshape((1,) + shape)  73.7 us
    ppermute x15, starting transfers between devices, line_scatter(): rising = lax.ppermute(upward.astype(BF), 'head', up)  66.6 us
    ppermute x18, waiting for transfers between devices, line_gather(): falling = lax.ppermute(falling, 'head', down)  52.7 us
    ppermute x18, waiting for transfers between devices, line_gather(): rising = lax.ppermute(rising, 'head', up)  49 us
  transfers between devices with their start and end apart: 116, of which 28 were waited for; matrix products, arithmetic and copies ran while one was open for 39% of the time, Pallas kernels for 14%

profile of v1, /device:TPU:1, one launch (start us, length us, event | category | flops | bytes accessed | tf_op | source)
XLA Modules:
  0.0 1342.4 jit_solution(17492229264414012361)
XLA Ops:
  18.5 14.3 %collective-permute-done = bf16[2,256,768]{2,1,0:T(8,128)(2,1)} collective-permute-done((bf16[2,256,768]{2,1,0:T(8,128)(2,1)}, bf16[2,256,768]{2,1,0:T(8,128)(2,1)}, u32[]{:S(2)}, u32[]{:S(2)}) %collective-permute-start) | collective-permute-done | bytes 786464 | tf_op jit(solution)/shard_map/ppermute | solution.py:50
  44.9 21.3 %all_gather.22 = bf16[768,576]{0,1:T(8,128)(2,1)S(1)} all-gather(bf16[384,576]{0,1:T(8,128)(2,1)S(1)} %bitcast.189), channel_id=1, replica_groups=mesh['fsdp'=2,'ctx'=4,'head'=4] {'fsdp'}, dimensions={0}, use_global_device_ids=true | all-gather | bytes 1327104 | tf_op jit(solution)/shard_map/all_gather | solution.py:26
  93.9 9.5 collective-permute-done.5
  120.9 24.6 %collective-permute-done.7 = bf16[2,1024,384]{2,1,0:T(8,128)(2,1)} collective-permute-done((bf16[2,1024,384]{2,1,0:T(8,128)(2,1)}, bf16[2,1024,384]{2,1,0:T(8,128)(2,1)}, u32[]{:S(2)}, u32[]{:S(2)}) %collective-permute-start.7) | collective-permute-done | bytes 1572896 | tf_op jit(solution)/shard_map/ppermute | solution.py:22
  182.1 37.6 %attend_forward.1 = (f32[2,1024,192]{2,1,0:T(8,128)}, bf16[2,1024,192]{2,1,0:T(8,128)(2,1)S(1)}, f32[2,1024,128]{2,1,0:T(8,128)S(1)}) custom-call(s32[1]{0:T(128)} %bitcast.2.ctx_ref, s32[2,4,4]{2,1,0:T(4,128)S(1)} %pad_add_fusion.1.bounds_ref, bf16[2,1024,192]{2,1,0:T(8,128)(2,1)S(1)} %copy-done.5, bf16[4,2,1024,384]{3,2,1,0:T(8,128)(2,1)} %pad_maximum_fusion.kv_ref, ...), custom_call_target="tpu_custom_call" | custom-call | flops 22548578304 | bytes 16777216 | tf_op jit(solution)/shard_map/attend_forward/pallas_call | solution.py:176
  232.2 8.7 all_gather.25.refs_7_
  245.2 32.0 %collective-permute-start.10 = (bf16[512,768]{0,1:T(8,128)(2,1)}, bf16[512,768]{0,1:T(8,128)(2,1)}, u32[]{:S(2)}, u32[]{:S(2)}) collective-permute-start(bf16[512,768]{0,1:T(8,128)(2,1)} %multiply_convert_fusion.1), channel_id=1, source_target_pairs={{0,8},{4,12},{8,0},{12,4},{1,9},{5,13},{9,1},{13,5},{2,10},{6,14},... | collective-permute-start | bytes 2359304 | tf_op jit(solution)/shard_map/ppermute | solution.py:22
  283.7 11.3 collective-permute-done.10
  317.9 84.6 %gated_mlp.2 = (f32[2048,768]{1,0:T(8,128)}, f32[2048,768]{1,0:T(8,128)}, f32[2048,1]{1,0:T(8,128)}, bf16[2,768,2048]{2,1,0:T(8,128)(2,1)}, bf16[2048,768]{1,0:T(8,128)(2,1)}) custom-call(bf16[2048,768]{1,0:T(8,128)(2,1)} %copy.233.refs_0_, bf16[768,2048]{1,0:T(8,128)(2,1)} %get-tuple-element.124.refs_1_, bf16[2048,768]{1,0:T(8,128)(2,1)} %copy.234.refs_2_, ...), custom_call_target="tpu_custom_call" | custom-call | flops 57982058496 | bytes 41943040 | tf_op jit(solution)/shard_map/gated_mlp/pallas_call | solution.py:377
  407.2 32.6 %gated_mlp.3 = (f32[2048,768]{1,0:T(8,128)}, f32[2048,768]{1,0:T(8,128)}, f32[2048,1]{1,0:T(8,128)}, bf16[2,768,512]{2,1,0:T(8,128)(2,1)}, bf16[512,768]{1,0:T(8,128)(2,1)}) custom-call(bf16[2048,768]{1,0:T(8,128)(2,1)} %copy.233.refs_0_, bf16[768,2048]{1,0:T(8,128)(2,1)} %get-tuple-element.124.refs_1_, bf16[2048,768]{1,0:T(8,128)(2,1)} %copy.234.refs_2_, ...), custom_call_target="tpu_custom_call" | custom-call | flops 14495514624 | bytes 41943040 | tf_op jit(solution)/shard_map/gated_mlp/pallas_call | solution.py:377
  590.8 16.1 %collective-permute-done.55 = bf16[2,96,512]{2,1,0:T(8,128)(2,1)S(1)} collective-permute-done((bf16[2,96,512]{2,1,0:T(8,128)(2,1)}, bf16[2,96,512]{2,1,0:T(8,128)(2,1)S(1)}, u32[]{:S(2)}, u32[]{:S(2)}) %collective-permute-start.55) | collective-permute-done | bytes 196640 | tf_op jit(solution)/shard_map/ppermute | solution.py:51
  641.5 35.7 %attend_backward.1 = (f32[2,1024,192]{2,1,0:T(8,128)S(1)}, bf16[4,2,1024,384]{3,2,1,0:T(8,128)(2,1)}) custom-call(s32[1]{0:T(128)} %bitcast.2.ctx_ref, s32[2,8,2]{2,1,0:T(8,128)S(1)} %pad_add_fusion.bounds_ref, s32[2,2]{1,0:T(2,128)S(1)} %slice.182.edges_ref, bf16[2,1024,192]{2,1,0:T(8,128)(2,1)S(1)} %copy-done.6, ...), custom_call_target="tpu_custom_call" | custom-call | flops 56371445760 | bytes 33554432 | tf_op jit(solution)/shard_map/attend_backward/pallas_call | solution.py:266
  686.7 25.1 %collective-permute-start.58 = (bf16[2,384,512]{2,1,0:T(8,128)(2,1)}, bf16[2,384,512]{2,1,0:T(8,128)(2,1)}, u32[]{:S(2)}, u32[]{:S(2)}) collective-permute-start(bf16[2,384,512]{2,1,0:T(8,128)(2,1)} %constant_dynamic-slice_fusion.13), channel_id=1, source_target_pairs={{0,8},{4,12},{8,0},{12,4},{1,9},{5,13},{9,1},{13,5},{2,10},{6,14},... | collective-permute-start | bytes 2359304 | tf_op jit(solution)/shard_map/ppermute | solution.py:22
  726.2 21.4 %collective-permute-done.99 = bf16[256,768]{1,0:T(8,128)(2,1)S(1)} collective-permute-done((bf16[256,768]{1,0:T(8,128)(2,1)S(1)}, bf16[256,768]{1,0:T(8,128)(2,1)S(1)}, u32[]{:S(2)}, u32[]{:S(2)}) %collective-permute-start.99) | collective-permute-done | bytes 393248 | tf_op jit(solution)/shard_map/ppermute | solution.py:50
  769.4 33.7 %dynamic_update_slice.48 = f32[4,2,384,2,256]{4,0,3,1,2:T(4,128)} dynamic-update-slice(f32[4,2,384,2,256]{4,0,3,1,2:T(4,128)} %broadcast_in_dim.82, f32[1,2,384,2,256]{4,0,3,1,2:T(1,128)} %copy.249, s32[]{:T(128)S(6)} %select_n.182, s32[]{:T(128)} %constant.133.clone.1, s32[]{:T(128)} %constant.133.clone.1, s32[]{:T(128)} %constant.133.clone.1, s32[]{:T(128)} %constant.133.clone.1) | dynamic-update-slice | bytes 3145732 | tf_op jit(solution)/shard_map/dynamic_update_slice | solution.py:615
  803.2 11.2 all-reduce.5.cloned.1.call-done
  844.5 33.5 %dynamic_update_slice.49 = f32[4,2,384,2,256]{4,0,3,1,2:T(4,128)} dynamic-update-slice(f32[4,2,384,2,256]{4,0,3,1,2:T(4,128)} %dynamic_update_slice.48, f32[1,2,384,2,256]{4,0,3,1,2:T(1,128)S(1)} %copy.250, s32[]{:T(128)S(6)} %select_n.203, s32[]{:T(128)} %constant.133.clone.1, s32[]{:T(128)} %constant.133.clone.1, s32[]{:T(128)} %constant.133.clone.1, s32[]{:T(128)} %constant.133.clone.1) | dynamic-update-slice | bytes 3145732 | tf_op jit(solution)/shard_map/dynamic_update_slice | solution.py:615
  878.0 33.5 %dynamic_update_slice.50 = f32[4,2,384,2,256]{4,0,3,1,2:T(4,128)} dynamic-update-slice(f32[4,2,384,2,256]{4,0,3,1,2:T(4,128)} %dynamic_update_slice.49, f32[1,2,384,2,256]{4,0,3,1,2:T(1,128)S(1)} %copy.251, s32[]{:T(128)S(6)} %select_n.204, s32[]{:T(128)} %constant.133.clone.1, s32[]{:T(128)} %constant.133.clone.1, s32[]{:T(128)} %constant.133.clone.1, s32[]{:T(128)} %constant.133.clone.1) | dynamic-update-slice | bytes 3145732 | tf_op jit(solution)/shard_map/dynamic_update_slice | solution.py:615
  915.4 33.5 %dynamic_update_slice.51 = f32[4,2,384,2,256]{4,0,3,1,2:T(4,128)} dynamic-update-slice(f32[4,2,384,2,256]{4,0,3,1,2:T(4,128)} %dynamic_update_slice.50, f32[1,2,384,2,256]{4,0,3,1,2:T(1,128)S(1)} %copy.252, s32[]{:T(128)S(6)} %select_n.205, s32[]{:T(128)} %constant.133.clone.1, s32[]{:T(128)} %constant.133.clone.1, s32[]{:T(128)} %constant.133.clone.1, s32[]{:T(128)} %constant.133.clone.1) | dynamic-update-slice | bytes 3145732 | tf_op jit(solution)/shard_map/dynamic_update_slice | solution.py:615
  948.9 8.2 reshape.558
  1064.2 20.3 %all-reduce.3.cloned.1.call-done = bf16[384,1,576]{0,2,1:T(8,128)(2,1)} async-done(((bf16[384,1,576]{0,2,1:T(8,128)(2,1)}), bf16[384,1,576]{0,2,1:T(8,128)(2,1)}) %all-reduce.3.cloned.1.call-update) | async-done | bytes 442384 | tf_op jit(solution)/shard_map/psum | solution.py:629
  1090.3 41.0 %psum.21 = f32[6,768]{1,0:T(8,128)S(1)} all-reduce(f32[6,768]{1,0:T(8,128)S(1)} %pad_maximum_fusion.8), channel_id=1, replica_groups=mesh['fsdp'=2,'ctx'=4,'head'=4] {'fsdp','ctx','head'}, use_global_device_ids=true, to_apply=%region_13.14 | all-reduce | flops 4608 | bytes 36864 | tf_op jit(solution)/shard_map/psum | solution.py:635
  1165.1 13.6 %collective-permute-done.88 = bf16[2,96,2048]{2,1,0:T(8,128)(2,1)S(1)} collective-permute-done((bf16[2,96,2048]{2,1,0:T(8,128)(2,1)}, bf16[2,96,2048]{2,1,0:T(8,128)(2,1)S(1)}, u32[]{:S(2)}, u32[]{:S(2)}) %collective-permute-start.88) | collective-permute-done | bytes 786464 | tf_op jit(solution)/shard_map/ppermute | solution.py:51
  1226.3 12.1 broadcast_in_dim.84
  (624 shorter events, 709.9 us)
Async XLA Ops:
  7.2 234.1 %all-gather.7.cloned.1.call-start = ((), (), s32[]{:S(2)}) async-start(), calls=%async_computation.2 | async-start | bytes 1769472 | tf_op jit(solution)/shard_map/all_gather | solution.py:26
  7.9 309.9 %all-gather.13.cloned.1.call-start = ((), (), s32[]{:S(2)}) async-start(), calls=%async_computation.7 | async-start | bytes 4718592 | tf_op jit(solution)/shard_map/all_gather | solution.py:26
  10.7 307.2 %all-gather.11.cloned.1.call-start = ((), (), s32[]{:S(2)}) async-start(), calls=%async_computation.6 | async-start | bytes 9437184 | tf_op jit(solution)/shard_map/all_gather | solution.py:26
  41.8 364.4 %all-gather.9.cloned.1.call-start = ((), (), s32[]{:S(2)}) async-start(), calls=%async_computation.3 | async-start | bytes 2359296 | tf_op jit(solution)/shard_map/all_gather | solution.py:26
  155.5 121.7 %collective-permute-start.12 = (bf16[512,768]{0,1:T(8,128)(2,1)}, bf16[512,768]{0,1:T(8,128)(2,1)}, u32[]{:S(2)}, u32[]{:S(2)}) collective-permute-start(bf16[512,768]{0,1:T(8,128)(2,1)} %bitcast.96), channel_id=1, source_target_pairs={{0,4},{4,0},{8,12},{12,8},{1,5},{5,1},{9,13},{13,9},{2,6},{6,2},{1... | collective-permute-start | bytes 2359304 | tf_op jit(solution)/shard_map/ppermute | solution.py:22
  155.5 85.5 %collective-permute-start.13 = (bf16[512,768]{0,1:T(8,128)(2,1)}, bf16[512,768]{0,1:T(8,128)(2,1)}, u32[]{:S(2)}, u32[]{:S(2)}) collective-permute-start(bf16[512,768]{0,1:T(8,128)(2,1)} %bitcast.96), channel_id=1, source_target_pairs={{0,8},{4,12},{8,0},{12,4},{1,9},{5,13},{9,1},{13,5},{2,10},{6,14},... | collective-permute-start | bytes 2359304 | tf_op jit(solution)/shard_map/ppermute | solution.py:22
  460.3 81.1 %collective-permute-start.21 = (bf16[512,768]{0,1:T(8,128)(2,1)S(1)}, bf16[512,768]{0,1:T(8,128)(2,1)S(1)}, u32[]{:S(2)}, u32[]{:S(2)}) collective-permute-start(bf16[512,768]{0,1:T(8,128)(2,1)S(1)} %get-tuple-element.120), channel_id=1, source_target_pairs={{0,4},{4,0},{8,12},{12,8},{1,5},{5,1},{9,13},{13,9},{2,6},{6,2},{1... | collective-permute-start | bytes 2359304 | tf_op jit(solution)/shard_map/ppermute | solution.py:22
  536.3 144.8 %collective-permute-start.76 = (bf16[2,384,2048]{2,1,0:T(8,128)(2,1)}, bf16[2,384,2048]{2,1,0:T(8,128)(2,1)}, u32[]{:S(2)}, u32[]{:S(2)}) collective-permute-start(bf16[2,384,2048]{2,1,0:T(8,128)(2,1)} %constant_dynamic-slice_fusion.8), channel_id=1, source_target_pairs={{0,16},{16,0},{1,17},{17,1},{2,18},{18,2},{3,19},{19,3},{4,20},{20... | collective-permute-start | bytes 9437192 | tf_op jit(solution)/shard_map/ppermute | solution.py:22
  547.3 167.4 %collective-permute-start.73 = (bf16[256,768]{1,0:T(8,128)(2,1)}, bf16[256,768]{1,0:T(8,128)(2,1)}, u32[]{:S(2)}, u32[]{:S(2)}) collective-permute-start(bf16[256,768]{1,0:T(8,128)(2,1)} %get-tuple-element.100), channel_id=1, source_target_pairs={{0,4},{4,0},{8,12},{12,8},{1,5},{5,1},{9,13},{13,9},{2,6},{6,2},{1... | collective-permute-start | bytes 1179656 | tf_op jit(solution)/shard_map/ppermute | solution.py:22
  580.3 234.1 %all-reduce.5.cloned.1.call-start = ((), (), s32[]{:S(2)}) async-start(), calls=%async_computation.5 | async-start | bytes 1179648 | tf_op jit(solution)/shard_map/psum | solution.py:633
  622.9 96.7 %collective-permute-start.43 = (bf16[384,768]{1,0:T(8,128)(2,1)}, bf16[384,768]{1,0:T(8,128)(2,1)}, u32[]{:S(2)}, u32[]{:S(2)}) collective-permute-start(bf16[384,768]{1,0:T(8,128)(2,1)} %constant_dynamic-slice_fusion.17), channel_id=1, source_target_pairs={{0,16},{16,0},{1,17},{17,1},{2,18},{18,2},{3,19},{19,3},{4,20},{20... | collective-permute-start | bytes 1769480 | tf_op jit(solution)/shard_map/ppermute | solution.py:22
  713.0 248.2 %collective-permute-start.28 = (bf16[2,1024,384]{2,1,0:T(8,128)(2,1)}, bf16[2,1024,384]{2,1,0:T(8,128)(2,1)}, u32[]{:S(2)}, u32[]{:S(2)}) collective-permute-start(bf16[2,1024,384]{2,1,0:T(8,128)(2,1)} %get-tuple-element.111), channel_id=1, source_target_pairs={{0,4},{4,0},{8,12},{12,8},{1,5},{5,1},{9,13},{13,9},{2,6},{6,2},{1... | collective-permute-start | bytes 4718600 | tf_op jit(solution)/shard_map/ppermute | solution.py:22
  714.7 104.4 %collective-permute-start.77 = (bf16[2,96,2048]{2,1,0:T(8,128)(2,1)}, bf16[2,96,2048]{2,1,0:T(8,128)(2,1)}, u32[]{:S(2)}, u32[]{:S(2)}) collective-permute-start(bf16[2,96,2048]{2,1,0:T(8,128)(2,1)} %get-tuple-element.114), channel_id=1, source_target_pairs={{0,1},{1,2},{2,3},{4,5},{5,6},{6,7},{8,9},{9,10},{10,11},{12,13},{... | collective-permute-start | bytes 2359304 | tf_op jit(solution)/shard_map/ppermute | solution.py:76
  725.3 359.2 %all-reduce.3.cloned.1.call-start = ((), (), s32[]{:S(2)}) async-start(), calls=%async_computation.4 | async-start | bytes 884736 | tf_op jit(solution)/shard_map/psum | solution.py:629
  725.4 97.6 %collective-permute-start.57 = (bf16[2,384,512]{2,1,0:T(8,128)(2,1)}, bf16[2,384,512]{2,1,0:T(8,128)(2,1)}, u32[]{:S(2)}, u32[]{:S(2)}) collective-permute-start(bf16[2,384,512]{2,1,0:T(8,128)(2,1)} %constant_dynamic-slice_fusion.13), channel_id=1, source_target_pairs={{0,4},{4,0},{8,12},{12,8},{1,5},{5,1},{9,13},{13,9},{2,6},{6,2},{1... | collective-permute-start | bytes 2359304 | tf_op jit(solution)/shard_map/ppermute | solution.py:22
  726.1 98.1 %collective-permute-start.59 = (bf16[2,384,512]{2,1,0:T(8,128)(2,1)}, bf16[2,384,512]{2,1,0:T(8,128)(2,1)}, u32[]{:S(2)}, u32[]{:S(2)}) collective-permute-start(bf16[2,384,512]{2,1,0:T(8,128)(2,1)} %collective-permute-done.58), channel_id=1, source_target_pairs={{0,4},{4,0},{8,12},{12,8},{1,5},{5,1},{9,13},{13,9},{2,6},{6,2},{1... | collective-permute-start | bytes 2359304 | tf_op jit(solution)/shard_map/ppermute | solution.py:22
  819.1 138.0 %collective-permute-start.103 = (bf16[256,768]{1,0:T(8,128)(2,1)}, bf16[256,768]{1,0:T(8,128)(2,1)}, u32[]{:S(2)}, u32[]{:S(2)}) collective-permute-start(bf16[256,768]{1,0:T(8,128)(2,1)} %collective-permute-done.102), channel_id=1, source_target_pairs={{1,0},{2,1},{3,2},{5,4},{6,5},{7,6},{9,8},{10,9},{11,10},{13,12},{... | collective-permute-start | bytes 1179656 | tf_op jit(solution)/shard_map/ppermute | solution.py:51
  823.0 144.3 %collective-permute-start.80 = (bf16[2,96,2048]{2,1,0:T(8,128)(2,1)}, bf16[2,96,2048]{2,1,0:T(8,128)(2,1)}, u32[]{:S(2)}, u32[]{:S(2)}) collective-permute-start(bf16[2,96,2048]{2,1,0:T(8,128)(2,1)} %get-tuple-element.115), channel_id=1, source_target_pairs={{1,0},{2,1},{3,2},{5,4},{6,5},{7,6},{9,8},{10,9},{11,10},{13,12},{... | collective-permute-start | bytes 2359304 | tf_op jit(solution)/shard_map/ppermute | solution.py:77
  824.3 143.0 %collective-permute-start.78 = (bf16[2,96,2048]{2,1,0:T(8,128)(2,1)}, bf16[2,96,2048]{2,1,0:T(8,128)(2,1)}, u32[]{:S(2)}, u32[]{:S(2)}) collective-permute-start(bf16[2,96,2048]{2,1,0:T(8,128)(2,1)} %add_convert_fusion.7), channel_id=1, source_target_pairs={{0,1},{1,2},{2,3},{4,5},{5,6},{6,7},{8,9},{9,10},{10,11},{12,13},{... | collective-permute-start | bytes 2359304 | tf_op jit(solution)/shard_map/ppermute | solution.py:76
  829.8 135.1 %collective-permute-start.101 = (bf16[256,768]{1,0:T(8,128)(2,1)}, bf16[256,768]{1,0:T(8,128)(2,1)}, u32[]{:S(2)}, u32[]{:S(2)}) collective-permute-start(bf16[256,768]{1,0:T(8,128)(2,1)} %collective-permute-done.100), channel_id=1, source_target_pairs={{0,1},{1,2},{2,3},{4,5},{5,6},{6,7},{8,9},{9,10},{10,11},{12,13},{... | collective-permute-start | bytes 1179656 | tf_op jit(solution)/shard_map/ppermute | solution.py:50
  983.3 77.6 %collective-permute-start.106 = (bf16[1024,768]{1,0:T(8,128)(2,1)}, bf16[1024,768]{1,0:T(8,128)(2,1)}, u32[]{:S(2)}, u32[]{:S(2)}) collective-permute-start(bf16[1024,768]{1,0:T(8,128)(2,1)} %get-tuple-element.96), channel_id=1, source_target_pairs={{0,8},{4,12},{8,0},{12,4},{1,9},{5,13},{9,1},{13,5},{2,10},{6,14},... | collective-permute-start | bytes 4718600 | tf_op jit(solution)/shard_map/ppermute | solution.py:22
  1045.5 87.1 %collective-permute-start.30 = (bf16[2,256,768]{2,1,0:T(8,128)(2,1)}, bf16[2,256,768]{2,1,0:T(8,128)(2,1)}, u32[]{:S(2)}, u32[]{:S(2)}) collective-permute-start(bf16[2,256,768]{2,1,0:T(8,128)(2,1)} %get-tuple-element.118), channel_id=1, source_target_pairs={{0,1},{1,2},{2,3},{4,5},{5,6},{6,7},{8,9},{9,10},{10,11},{12,13},{... | collective-permute-start | bytes 2359304 | tf_op jit(solution)/shard_map/ppermute | solution.py:76
  1052.1 88.9 %collective-permute-start.87 = (bf16[2,96,2048]{2,1,0:T(8,128)(2,1)}, bf16[2,96,2048]{2,1,0:T(8,128)(2,1)}, u32[]{:S(2)}, u32[]{:S(2)}) collective-permute-start(bf16[2,96,2048]{2,1,0:T(8,128)(2,1)} %collective-permute-done.86), channel_id=1, source_target_pairs={{1,0},{2,1},{3,2},{5,4},{6,5},{7,6},{9,8},{10,9},{11,10},{13,12},{... | collective-permute-start | bytes 2359304 | tf_op jit(solution)/shard_map/ppermute | solution.py:51
  1055.9 86.4 %collective-permute-start.85 = (bf16[2,96,2048]{2,1,0:T(8,128)(2,1)}, bf16[2,96,2048]{2,1,0:T(8,128)(2,1)}, u32[]{:S(2)}, u32[]{:S(2)}) collective-permute-start(bf16[2,96,2048]{2,1,0:T(8,128)(2,1)} %collective-permute-done.84), channel_id=1, source_target_pairs={{0,1},{1,2},{2,3},{4,5},{5,6},{6,7},{8,9},{9,10},{10,11},{12,13},{... | collective-permute-start | bytes 2359304 | tf_op jit(solution)/shard_map/ppermute | solution.py:50
  (160 other events, 3657.0 us)
Sparse Core Ops, SparseCore 0:
  9.6 24.8 all-gather.6
  36.0 54.5 all-gather.12
  92.7 79.5 all-gather.10
  173.7 27.1 all-gather.8
  725.5 88.8 all-reduce.4
  1052.2 32.2 all-reduce.2

commit v2 on v1

v2 whole, which is shorter than its diff:
```python
import functools
import math

import jax
import jax.numpy as jnp
from jax import lax
from jax.experimental import pallas as pl
from jax.experimental.pallas import tpu as pltpu
from jax.sharding import PartitionSpec as P

HEAD_DIM = 64
EPS = 1e-06
NEG = -1e30
ROPE_BASE = 10000.0
BF = jnp.bfloat16
F32 = jnp.float32
MB = 1 << 20


def swap_with(value, axis_name, bit):
    size = lax.axis_size(axis_name)
    return lax.ppermute(value, axis_name, [(i, i ^ bit) for i in range(size)])


def fsdp_gather(value, axis):
    return lax.all_gather(value, "fsdp", axis=axis, tiled=True)


def fsdp_gather_small(value, axis):
    if lax.axis_size("fsdp") != 2:
        return fsdp_gather(value, axis)
    other = swap_with(value, "fsdp", 1)
    first = lax.axis_index("fsdp") == 0
    return jnp.where(
        first, jnp.concatenate([value, other], axis=axis), jnp.concatenate([other, value], axis=axis)
    )


def line_gather(value, axis):
    count = lax.axis_size("head")
    mine = lax.axis_index("head")
    part = value.shape[axis]
    up = [(i, i + 1) for i in range(count - 1)]
    down = [(i + 1, i) for i in range(count - 1)]
    below, above = [], []
    rising, falling = value, value
    for _ in range(count - 1):
        rising = lax.ppermute(rising, "head", up)
        falling = lax.ppermute(falling, "head", down)
        below.insert(0, rising)
        above.append(falling)
    line = jnp.concatenate(below + [value] + above, axis=axis)
    return lax.dynamic_slice_in_dim(line, (count - 1 - mine) * part, count * part, axis)


def line_scatter(value, axis):
    count = lax.axis_size("head")
    mine = lax.axis_index("head")
    part = value.shape[axis] // count
    up = [(i, i + 1) for i in range(count - 1)]
    down = [(i + 1, i) for i in range(count - 1)]

    def block(index):
        index = jnp.clip(index, 0, count - 1)
        return lax.dynamic_slice_in_dim(value, index * part, part, axis).astype(F32)

    rising, falling = None, None
    for step in range(count - 1):
        upward = block(count - 1 - step + mine)
        downward = block(step - (count - 1) + mine)
        if step:
            upward = upward + rising.astype(F32)
            downward = downward + falling.astype(F32)
        rising = lax.ppermute(upward.astype(BF), "head", up)
        falling = lax.ppermute(downward.astype(BF), "head", down)
    return block(mine) + rising.astype(F32) + falling.astype(F32)


def after(value, *others):
    return lax.optimization_barrier((value, *others))[0] if others else value


def corner(value):
    return lax.slice(value, (0,) * value.ndim, (1,) * value.ndim)


def paired():
    return lax.axis_size("fsdp") == 2


def group_member():
    ctx = lax.axis_index("ctx")
    return (ctx // 2) * 2 + lax.axis_index("fsdp") if paired() else ctx


def group_swap(value, bit):
    if paired() and bit == 1:
        return swap_with(value, "fsdp", 1)
    return swap_with(value, "ctx", bit)


def group_gather(value):
    half = value.shape[0] // 2
    one, two = group_swap(value, 1), group_swap(value, 2)
    far = jnp.concatenate([group_swap(one[:half], 2), group_swap(two[half:], 1)], axis=0)
    return [value, one, two, far]


def group_scatter_near(blocks):
    own, one, two, far = blocks
    half = far.shape[0] // 2
    by_one, by_two = group_swap(far[:half], 1), group_swap(far[half:], 2)
    two = jnp.concatenate([(two[:half].astype(F32) + by_one.astype(F32)).astype(BF), two[half:]], axis=0)
    one = jnp.concatenate([one[:half], (one[half:].astype(F32) + by_two.astype(F32)).astype(BF)], axis=0)
    return own, one, two


def group_scatter(blocks):
    own, one, two = group_scatter_near(blocks)
    return own.astype(F32) + group_swap(one, 1).astype(F32) + group_swap(two, 2).astype(F32)


def half_sum(value, axis, axis_name, bit_value, bit):
    part = value.shape[axis] // 2
    sent = lax.dynamic_slice_in_dim(value, (1 - bit_value) * part, part, axis)
    kept = lax.dynamic_slice_in_dim(value, bit_value * part, part, axis)
    got = swap_with(sent, axis_name, bit)
    return kept.astype(F32) + got.astype(F32)


def pack(d_in, d_out, parts, wide):
    packed = []
    for d in (d_in, d_out):
        j, r, w = d.shape
        d = d.reshape(j, parts, r // parts, w // wide, wide).transpose(1, 0, 3, 2, 4)
        packed.append(d.reshape(parts, j, -1, wide))
    return jnp.concatenate(packed, axis=2)


def sum_parts(one, two, more=None):
    wide = 256
    groups, shards = lax.axis_size("head"), lax.axis_size("fsdp")
    if paired():
        parts, over = groups, "head"
        packed = one.astype(F32) + swap_with(two, "ctx", 1).astype(F32)
        packed = packed.astype(BF).reshape(parts, -1, wide)
        if more is not None:
            more = half_sum(more, 1, "ctx", lax.axis_index("ctx") % 2, 1).astype(BF)
    else:
        parts, over = groups * shards, ("fsdp", "head")
        packed = pack(one, two, parts, wide).reshape(parts, -1, wide)
    if more is not None:
        j, r, w = more.shape
        more = more.reshape(j, parts, r // parts, w // wide, wide).transpose(1, 0, 3, 2, 4)
        packed = jnp.concatenate([packed, more.reshape(parts, -1, wide)], axis=1)
    packed = packed.reshape(-1, wide)
    return lax.psum_scatter(packed, over, scatter_dimension=0, tiled=True)


def exchange_parts(part):
    if not paired():
        return part
    core, shard = lax.axis_index("ctx") % 2, lax.axis_index("fsdp")
    ctxs = lax.axis_size("ctx")
    moves = [(f * ctxs + c, (1 - f) * ctxs + (c ^ 1)) for f in range(2) for c in range(ctxs) if c % 2 != f]
    got = lax.ppermute(part, ("fsdp", "ctx"), moves)
    return jnp.where(core == shard, part, got)


def share_parts(part):
    whole = lax.all_gather(part, ("ctx", "head"), axis=0, tiled=False)
    return whole.reshape((lax.axis_size("ctx"), lax.axis_size("head")) + part.shape)


def ctx_gather(value):
    blocks = [value]
    bit = lax.axis_size("ctx") // 2
    found = {0: value}
    while bit:
        for k in list(found):
            found[k ^ bit] = swap_with(found[k], "ctx", bit)
        bit //= 2
    blocks = [found[k] for k in range(len(found))]
    return blocks


def ctx_scatter(blocks):
    held = {k: blocks[k] for k in range(len(blocks))}
    bit = 1
    while len(held) > 1:
        kept = {}
        for k in list(held):
            if not k & bit:
                got = swap_with(held[k | bit], "ctx", bit)
                kept[k] = held[k].astype(F32) + got.astype(F32)
        held = {k: (v if len(kept) == 1 else v.astype(BF)) for k, v in kept.items()}
        bit *= 2
    return held[0]


MESH_ID = pl.DeviceIdType.MESH


def enter(partners):
    barrier = pltpu.get_barrier_semaphore()
    for there, device in partners:
        if there is None:
            pl.semaphore_signal(barrier, inc=1, device_id=device, device_id_type=MESH_ID)
        else:

            @pl.when(there)
            def _(device=device):
                pl.semaphore_signal(barrier, inc=1, device_id=device, device_id_type=MESH_ID)

    here = sum(1 if there is None else there.astype(jnp.int32) for there, _ in partners)
    pl.semaphore_wait(barrier, here)


def send(src, dst, sems, device):
    return pltpu.make_async_remote_copy(
        src_ref=src, dst_ref=dst, send_sem=sems[0], recv_sem=sems[1], device_id=device, device_id_type=MESH_ID
    )


def line_relay(place, z, count, up, down, up_sems, down_sems):
    def copy(b, device, sems):
        return send(place(b), place(b), (sems[0].at[b], sems[1].at[b]), device)

    def pass_on(far):
        low, high = z - far, z + far

        @pl.when((low >= 0) & (z < count - 1))
        def _():
            if far:
                copy(low, up, up_sems).wait_recv()
            copy(low, up, up_sems).start()

        @pl.when((high < count) & (z > 0))
        def _():
            if far:
                copy(high, down, down_sems).wait_recv()
            copy(high, down, down_sems).start()

    def last(b):
        @pl.when((b < z) & (z == count - 1))
        def _():
            copy(b, up, up_sems).wait_recv()

        @pl.when((b > z) & (z == 0))
        def _():
            copy(b, down, down_sems).wait_recv()

    def sent(b):
        @pl.when((b <= z) & (z < count - 1))
        def _():
            copy(b, up, up_sems).wait_send()

        @pl.when((b >= z) & (z > 0))
        def _():
            copy(b, down, down_sems).wait_send()

    blocks = range(count)
    run = [functools.partial(pass_on, far) for far in blocks]
    return run, [functools.partial(last, b) for b in blocks], [functools.partial(sent, b) for b in blocks]


def line_gather_kernel(value, cid):
    count = lax.axis_size("head")
    seqs, rows, width = value.shape

    def kernel(v_ref, o_ref, us, ur, ds, dr, local):
        z = lax.axis_index("head")
        up, down = {"head": jnp.minimum(z + 1, count - 1)}, {"head": jnp.maximum(z - 1, 0)}

        def place(b):
            return o_ref.at[:, pl.ds(pl.multiple_of(b * rows, rows), rows), :]

        own = pltpu.make_async_copy(v_ref, o_ref.at[:, pl.ds(pl.multiple_of(z * rows, rows), rows), :], local)
        own.start()
        enter([(z < count - 1, up), (z > 0, down)])
        own.wait()
        run, last, sent = line_relay(place, z, count, up, down, (us, ur), (ds, dr))
        for step in (*run, *last, *sent):
            step()

    any_space = pl.BlockSpec(memory_space=pltpu.VMEM)
    return pl.pallas_call(
        kernel,
        out_shape=jax.ShapeDtypeStruct((seqs, count * rows, width), value.dtype),
        in_specs=[any_space],
        out_specs=any_space,
        scratch_shapes=[pltpu.SemaphoreType.DMA((count,))] * 4 + [pltpu.SemaphoreType.DMA],
        compiler_params=pltpu.CompilerParams(
            collective_id=cid, has_side_effects=True, vmem_limit_bytes=16 * MB
        ),
        name="line_gather",
        cost_estimate=pl.CostEstimate(flops=0, bytes_accessed=180 * MB, transcendentals=0),
    )(value)


def tail_kernel(parts, grads, cid):
    count, rows, width = parts.shape
    high, wide = grads.shape
    half, quarter, eighth = high // 2, high // 4, high // 8

    def kernel(p_ref, g_ref, o_ref, q_ref, gain_ref, q_s, up_in, up_out, dn_in, dn_out, s1, r1, s2, r2, r3, *sems):
        us, ur, ds, dr, gus, gur, gds, gdr, xs, ys, cs, yg, cg = sems
        z, f, c = lax.axis_index("head"), lax.axis_index("fsdp"), lax.axis_index("ctx")
        core, upper = lax.rem(c, 2), lax.div(c, 2)
        up, down = {"head": jnp.minimum(z + 1, count - 1)}, {"head": jnp.maximum(z - 1, 0)}
        over_x = {"fsdp": 1 - f}
        over_core = {"ctx": upper * 2 + 1 - core}
        over_y = {"ctx": (1 - upper) * 2 + core}
        enter([(z < count - 1, up), (z > 0, down), (None, over_x), (None, over_core), (None, over_y)])

        def rise(d):
            return send(up_out.at[d], up_in.at[d], (us.at[d], ur.at[d]), up)

        def fall(d):
            return send(dn_out.at[d], dn_in.at[d], (ds.at[d], dr.at[d]), down)

        def rising(d):
            @pl.when(z < d)
            def _():
                @pl.when(z == 0)
                def _():
                    up_out[d] = p_ref[d]

                @pl.when(z > 0)
                def _():
                    rise(d).wait_recv()
                    up_out[d] = (p_ref[d].astype(F32) + up_in[d].astype(F32)).astype(BF)

                rise(d).start()

        def falling(d):
            @pl.when(z > d)
            def _():
                @pl.when(z == count - 1)
                def _():
                    dn_out[d] = p_ref[d]

                @pl.when(z < count - 1)
                def _():
                    fall(d).wait_recv()
                    dn_out[d] = (p_ref[d].astype(F32) + dn_in[d].astype(F32)).astype(BF)

                fall(d).start()

        by_x = send(g_ref.at[pl.ds(pl.multiple_of((1 - f) * half, half), half), :], r1, (xs.at[0], xs.at[1]), over_x)
        by_core = send(
            s1.at[pl.ds(pl.multiple_of((1 - core) * quarter, quarter), quarter), :], r2, (cs.at[0], cs.at[1]), over_core
        )
        by_y = send(
            s2.at[pl.ds(pl.multiple_of((1 - upper) * eighth, eighth), eighth), :], r3, (ys.at[0], ys.at[1]), over_y
        )
        by_x.start()
        at_low, at_high = z == 0, z == count - 1
        pl.when(at_low)(lambda: rising(count - 1))
        pl.when(at_high)(lambda: falling(0))
        by_x.wait_recv()
        s1[...] = (g_ref[pl.ds(pl.multiple_of(f * half, half), half), :].astype(F32) + r1[...].astype(F32)).astype(BF)
        by_core.start()
        by_core.wait_recv()
        mine = s1[pl.ds(pl.multiple_of(core * quarter, quarter), quarter), :]
        s2[...] = (mine.astype(F32) + r2[...].astype(F32)).astype(BF)
        by_y.start()
        by_y.wait_recv()
        mine = s2[pl.ds(pl.multiple_of(upper * eighth, eighth), eighth), :]
        q_s[core, upper, z] = (mine.astype(F32) + r3[...].astype(F32)).astype(BF)
        run, last, sent = line_relay(
            lambda b: q_s.at[core, upper, b], z, count, up, down, (gus, gur), (gds, gdr)
        )
        run[0]()
        for d in range(1, count - 1):
            pl.when(at_low)(lambda d=d: rising(count - 1 - d))
            pl.when(at_high)(lambda d=d: falling(d))
        pl.when(jnp.logical_not(at_low))(lambda: rising(count - 1))
        run[1]()
        pl.when(jnp.logical_not(at_high))(lambda: falling(0))
        run[2]()
        for d in range(1, count - 1):
            pl.when(jnp.logical_not(at_low))(lambda d=d: rising(count - 1 - d))
            pl.when(jnp.logical_not(at_high))(lambda d=d: falling(d))
        for step in (*run[3:], *last):
            step()
        to_y = send(q_s.at[core, upper], q_s.at[core, upper], (yg.at[0], yg.at[1]), over_y)
        to_y.start()

        total = p_ref[z].astype(F32)
        o_ref[...] = total

        @pl.when(z > 0)
        def _():
            rise(z).wait_recv()
            o_ref[...] += up_in[z].astype(F32)

        @pl.when(z < count - 1)
        def _():
            fall(z).wait_recv()
            o_ref[...] += dn_in[z].astype(F32)

        to_y.wait_recv()
        to_core = send(q_s.at[core], q_s.at[core], (cg.at[0], cg.at[1]), over_core)
        to_core.start()
        to_core.wait_recv()
        part = width // count
        for a in range(2):
            for b in range(2):
                at = slice((a * 2 + b) * eighth, (a * 2 + b + 1) * eighth)
                gain = jnp.zeros((eighth, 128), F32)
                for n in range(count):
                    block = q_s[a, b, n].astype(F32)
                    for t in range(3):
                        col = t * width + n * part
                        q_ref[at, col : col + part] = block[:, t * part : (t + 1) * part]
                    gain += block[:, wide - 128 :]
                gain_ref[at, :] = gain
        for d in range(count):

            @pl.when(z < d)
            def _(d=d):
                rise(d).wait_send()

            @pl.when(z > d)
            def _(d=d):
                fall(d).wait_send()

        for step in sent:
            step()
        for copy in (by_x, by_core, by_y, to_y, to_core):
            copy.wait_send()

    vmem = pl.BlockSpec(memory_space=pltpu.VMEM)
    block = lambda *shape: pltpu.VMEM(shape, BF)
    return pl.pallas_call(
        kernel,
        out_shape=(
            jax.ShapeDtypeStruct((rows, width), F32),
            jax.ShapeDtypeStruct((half, 3 * width), F32),
            jax.ShapeDtypeStruct((half, 128), F32),
        ),
        in_specs=[vmem, vmem],
        out_specs=[vmem, vmem, vmem],
        scratch_shapes=[block(2, 2, count, eighth, wide)]
        + [block(count, rows, width)] * 4
        + [block(half, wide), block(half, wide), block(quarter, wide), block(quarter, wide), block(eighth, wide)]
        + [pltpu.SemaphoreType.DMA((count,))] * 8
        + [pltpu.SemaphoreType.DMA((2,))] * 5,
        compiler_params=pltpu.CompilerParams(
            collective_id=cid, has_side_effects=True, vmem_limit_bytes=40 * MB
        ),
        name="tail",
        cost_estimate=pl.CostEstimate(flops=0, bytes_accessed=220 * MB, transcendentals=0),
    )(parts, grads)


def dot_t(a, b):
    return lax.dot_general(a, b, (((1,), (1,)), ((), ())), preferred_element_type=F32)


def dot_l(a, b):
    return lax.dot_general(a, b, (((0,), (0,)), ((), ())), preferred_element_type=F32)


def dot(a, b):
    return jnp.dot(a, b, preferred_element_type=F32)


def attend_forward(words, bounds, queries, keys_values, starts, tq, tk, state):
    seqs, rows, width = queries.shape
    heads = width // HEAD_DIM
    blocks = keys_values.shape[0]
    per = rows // tk

    def kernel(word_ref, bounds_ref, q_ref, kv_ref, seg_ref, *refs):
        if state is None:
            acc_ref, row_ref = refs
        else:
            acc_in, row_in, o_ref, low_ref, lse_ref = refs
        s, i = pl.program_id(0), pl.program_id(1)
        here, first = word_ref[0], word_ref[1]
        seg = seg_ref[0]
        row_pos = here * rows + i * tq + lax.broadcasted_iota(jnp.int32, (tk, tq), 1)
        under = lax.broadcasted_iota(jnp.int32, (tk, tq), 0)

        def step(masked, t, carry):
            at = (lax.div(t, per) ^ here) - first
            off = pl.multiple_of(lax.rem(t, per) * tk, tk)
            new = []
            if masked:
                key_pos = t * tk + under
                seen = (key_pos <= row_pos) & (key_pos >= seg)
            for h in range(heads):
                top, total, acc = carry[3 * h : 3 * h + 3]
                cols = slice(h * HEAD_DIM, (h + 1) * HEAD_DIM)
                vals = slice(width + h * HEAD_DIM, width + (h + 1) * HEAD_DIM)
                scores = dot_t(kv_ref[at, 0, pl.ds(off, tk), cols], q_ref[0, :, cols])
                if masked:
                    scores = jnp.where(seen, scores, NEG)
                new_top = jnp.maximum(top, jnp.max(scores, axis=0, keepdims=True))
                weights = jnp.exp(scores - new_top)
                fade = jnp.exp(top - new_top)
                total = total * fade + jnp.sum(weights, axis=0, keepdims=True)
                acc = acc * fade + dot_l(kv_ref[at, 0, pl.ds(off, tk), vals], weights.astype(BF))
                new += [new_top, total, acc]
            return tuple(new)

        carry = []
        for h in range(heads):
            if state is None:
                carry += [jnp.full((1, tq), NEG, F32), jnp.zeros((1, tq), F32), jnp.zeros((HEAD_DIM, tq), F32)]
            else:
                carry += [
                    row_in[0, h : h + 1, :],
                    row_in[0, heads + h : heads + h + 1, :],
                    acc_in[0, h * HEAD_DIM : (h + 1) * HEAD_DIM, :],
                ]
        carry = tuple(carry)
        b = [bounds_ref[s, i, n] for n in range(4)]
        carry = lax.fori_loop(b[0], b[1], functools.partial(step, True), carry)
        carry = lax.fori_loop(b[1], b[2], functools.partial(step, False), carry)
        carry = lax.fori_loop(b[2], b[3], functools.partial(step, True), carry)
        tops, totals, accs = carry[::3], carry[1::3], carry[2::3]
        filler = jnp.zeros((8 - 2 * heads, tq), F32)
        if state is None:
            acc_ref[0] = jnp.concatenate(accs, axis=0)
            row_ref[0] = jnp.concatenate([*tops, *totals, filler], axis=0)
        else:
            result = jnp.concatenate([acc / total for acc, total in zip(accs, totals)], axis=0).T
            o_ref[0] = result
            low_ref[0] = result.astype(BF)
            logs = [top + jnp.log(total) for top, total in zip(tops, totals)]
            lse_ref[0] = jnp.concatenate([*logs, *totals, filler], axis=0)

    rows_spec = pl.BlockSpec((1, tq, width), lambda s, i, *_: (s, i, 0))
    acc_spec = pl.BlockSpec((1, width, tq), lambda s, i, *_: (s, 0, i))
    stat_spec = pl.BlockSpec((1, 8, tq), lambda s, i, *_: (s, 0, i))
    stat_shape = jax.ShapeDtypeStruct((seqs, 8, rows), F32)
    if state is None:
        out_shape = (jax.ShapeDtypeStruct((seqs, width, rows), F32), stat_shape)
        more, out_specs = [], [acc_spec, stat_spec]
    else:
        shape = (seqs, rows, width)
        out_shape = (jax.ShapeDtypeStruct(shape, F32), jax.ShapeDtypeStruct(shape, BF), stat_shape)
        more, out_specs = [acc_spec, stat_spec], [rows_spec, rows_spec, stat_spec]
    return pl.pallas_call(
        kernel,
        out_shape=out_shape,
        grid_spec=pltpu.PrefetchScalarGridSpec(
            num_scalar_prefetch=2,
            grid=(seqs, rows // tq),
            in_specs=[
                rows_spec,
                pl.BlockSpec((blocks, 1, rows, 2 * width), lambda s, i, *_: (0, s, 0, 0)),
                pl.BlockSpec((1, 1, tq), lambda s, i, *_: (s, 0, i)),
                *more,
            ],
            out_specs=out_specs,
        ),
        compiler_params=pltpu.CompilerParams(vmem_limit_bytes=48 * MB),
        name="attend_forward",
        cost_estimate=pl.CostEstimate(
            flops=int(2 * 2 * seqs * heads * rows * rows * 2 * HEAD_DIM * 4),
            bytes_accessed=64 * MB,
            transcendentals=int(seqs * heads * rows * rows * 2),
        ),
    )(words, bounds, queries, keys_values, starts, *(state or ()))


def attend_backward(words, bounds, edges, queries, keys_values, grads, stats, starts, tq, tk):
    seqs, rows, width = queries.shape
    heads = width // HEAD_DIM
    blocks = keys_values.shape[0]
    per = rows // tk

    def kernel(word_ref, bounds_ref, edges_ref, q_ref, kv_ref, do_ref, stat_ref, seg_ref, dq_ref, dkv_ref, acc):
        s = pl.program_id(0)
        here = word_ref[0]
        t = word_ref[2] * per + pl.program_id(1)

        @pl.when(pl.program_id(1) == 0)
        def _():
            dq_ref[...] = jnp.zeros_like(dq_ref)

        acc[...] = jnp.zeros_like(acc)
        lane = lax.broadcasted_iota(jnp.int32, (tk, tq), 1)
        key_pos = t * tk + lax.broadcasted_iota(jnp.int32, (tk, tq), 0)

        def tile(masked, i):
            off = pl.multiple_of(i * tq, tq)
            if masked:
                row_pos = here * rows + off + lane
                seen = (key_pos <= row_pos) & (key_pos >= seg_ref[0, 0:1, pl.ds(off, tq)])
            for h in range(heads):
                cols = slice(h * HEAD_DIM, (h + 1) * HEAD_DIM)
                vals = slice(width + h * HEAD_DIM, width + (h + 1) * HEAD_DIM)
                q = q_ref[0, pl.ds(off, tq), cols]
                do = do_ref[0, pl.ds(off, tq), cols]
                k = kv_ref[0, 0, :, cols]
                v = kv_ref[0, 0, :, vals]
                scores = dot_t(k, q)
                weights = jnp.exp(scores - stat_ref[0, h : h + 1, pl.ds(off, tq)])
                if masked:
                    weights = jnp.where(seen, weights, 0.0)
                dweights = dot_t(v, do)
                dscores = weights * (dweights - stat_ref[0, heads + h : heads + h + 1, pl.ds(off, tq)])
                dscores = dscores.astype(BF)
                acc[h] += dot(dscores, q)
                acc[heads + h] += dot(weights.astype(BF), do)
                dq_ref[0, pl.ds(off, tq), cols] += dot_l(dscores, k)

        def step(i, carry):
            first = here * rows + i * tq
            clear = (edges_ref[s, i] <= t * tk) & (t * tk + tk - 1 <= first)

            @pl.when(clear)
            def _():
                tile(False, i)

            @pl.when(jnp.logical_not(clear))
            def _():
                tile(True, i)

            return carry

        lax.fori_loop(bounds_ref[s, t, 0], bounds_ref[s, t, 1], step, 0)
        dkv_ref[0, 0] = jnp.concatenate([acc[n] for n in range(2 * heads)], axis=1).astype(BF)

    at = lambda s, t, w, *_: (((w[2] + t // per) ^ w[0]) - w[1], s, t % per, 0)
    return pl.pallas_call(
        kernel,
        out_shape=(
            jax.ShapeDtypeStruct((seqs, rows, width), F32),
            jax.ShapeDtypeStruct((blocks, seqs, rows, 2 * width), BF),
        ),
        grid_spec=pltpu.PrefetchScalarGridSpec(
            num_scalar_prefetch=3,
            grid=(seqs, blocks * per),
            in_specs=[
                pl.BlockSpec((1, rows, width), lambda s, t, *_: (s, 0, 0)),
                pl.BlockSpec((1, 1, tk, 2 * width), at),
                pl.BlockSpec((1, rows, width), lambda s, t, *_: (s, 0, 0)),
                pl.BlockSpec((1, 8, rows), lambda s, t, *_: (s, 0, 0)),
                pl.BlockSpec((1, 1, rows), lambda s, t, *_: (s, 0, 0)),
            ],
            out_specs=[
                pl.BlockSpec((1, rows, width), lambda s, t, *_: (s, 0, 0)),
                pl.BlockSpec((1, 1, tk, 2 * width), at),
            ],
            scratch_shapes=[pltpu.VMEM((2 * heads, tk, HEAD_DIM), F32)],
        ),
        compiler_params=pltpu.CompilerParams(vmem_limit_bytes=48 * MB),
        name="attend_backward",
        cost_estimate=pl.CostEstimate(
            flops=int(5 * 2 * seqs * heads * rows * rows * 2 * HEAD_DIM * 4),
            bytes_accessed=100 * MB,
            transcendentals=int(seqs * heads * rows * rows * 2),
        ),
    )(words, bounds, edges, queries, keys_values, grads, stats, starts)


def gated_mlp(rows_in, grads, grads_t, gates, words, routed, shared, steps, s_steps, groups):
    block_rows, width = rows_in[0].shape
    n_rows = len(rows_in)
    count = block_rows * n_rows
    tile = 256
    chunk = min(512, count)
    all_steps = steps + s_steps
    pieces = [(piece, held, where) for where, lists in enumerate((routed, shared)) for held in (0, 1) for piece in lists[held]]

    def kernel(word_ref, *refs):
        row_refs, refs = refs[:n_rows], refs[n_rows:]
        d_ref, dt_ref, c_in = refs[:3]
        piece_refs, refs = refs[3 : 3 + len(pieces)], refs[3 + len(pieces) :]
        y_out, dx_out, dc_ref, one_ref, two_ref, x_ref, xt_ref, c_ref, y_ref, dx_ref, w_s, wt_s, wo_s, wot_s, a_s, g_s = refs
        j = pl.program_id(0)

        @pl.when(j == 0)
        def _():
            dc_ref[...] = jnp.zeros_like(dc_ref)
            c_ref[...] = c_in[...]
            y_ref[...] = jnp.zeros_like(y_ref)
            dx_ref[...] = jnp.zeros_like(dx_ref)
            for n, ref in enumerate(row_refs):
                at = slice(n * block_rows, (n + 1) * block_rows)
                x_ref[at, :] = ref[...]
                xt_ref[:, at] = ref[...].T

        @pl.when(j == steps)
        def _():
            c_ref[...] = jnp.ones_like(c_ref)

        def fill(kind):
            for ref, (piece, held, where) in zip(piece_refs, pieces):
                if where != kind:
                    continue
                tall, wide = ref.shape
                row, times, lane_word, lane_times, lane = piece[3:]
                at = pl.ds(pl.multiple_of(word_ref[row], times), tall)
                if lane_word is None:
                    lanes = slice(lane, lane + wide)
                else:
                    lanes = pl.ds(pl.multiple_of(word_ref[lane_word], lane_times), wide)
                (w_s, wo_s)[held][at, lanes] = ref[...]

        pl.when(j < steps)(lambda: fill(0))
        pl.when(j >= steps)(lambda: fill(1))
        wt_s[...] = w_s[...].T
        wot_s[...] = wo_s[...].T

        routed_here = jnp.where(j < steps, 1.0, 0.0)

        def body(n, carry):
            at = pl.ds(pl.multiple_of(n * chunk, chunk), chunk)
            both = dot(x_ref[at, :], w_s[...])
            gate, up = both[:, :tile], both[:, tile:]
            raw = dot(d_ref[at, :], wot_s[...])
            c = c_ref[at, :]
            sig = 0.5 + 0.5 * jnp.tanh(0.5 * gate)
            silu = gate * sig
            act = silu * up

            dc_ref[at, :] += jnp.sum(act * raw, axis=1, keepdims=True) * routed_here
            back = raw * c
            a_low = (act * c).astype(BF)
            dg = (back * up * (sig + silu * (1.0 - sig))).astype(BF)
            du = (back * silu).astype(BF)
            a_s[at, :] = a_low
            g_s[at, :tile] = dg
            g_s[at, tile:] = du
            y_ref[at, :] += dot(a_low, wo_s[...])
            dx_ref[at, :] += dot(g_s[at, :], wt_s[...])
            return carry

        lax.fori_loop(0, count // chunk, body, 0)

        if groups:
            keep = word_ref[1]
            half = width // 2
            r, q = half // groups, tile // 2 // groups
            for ref, which in ((one_ref, keep), (two_ref, 1 - keep)):
                got = dot(xt_ref[pl.ds(pl.multiple_of(which * half, half), half), :], g_s[...]).astype(BF)
                for z in range(groups):
                    for g in range(2):
                        ref[z, 0, g * r : (g + 1) * r, :] = got[z * r : (z + 1) * r, g * tile : (g + 1) * tile]
            for n in range(width // tile):
                got = dot(dt_ref[n * tile : (n + 1) * tile, :], a_s[...]).T.astype(BF)
                low, high = got[: tile // 2], got[tile // 2 :]
                for ref, which in ((one_ref, keep), (two_ref, 1 - keep)):
                    mine = jnp.where(which == 0, low, high)
                    for z in range(groups):
                        ref[z, 0, 2 * r + n * q : 2 * r + (n + 1) * q, :] = mine[z * q : (z + 1) * q]
        else:
            one_ref[0] = dot(xt_ref[...], g_s[...]).astype(BF)
            for n in range(width // tile):
                at = slice(n * tile, (n + 1) * tile)
                two_ref[0, :, at] = dot(dt_ref[at, :], a_s[...]).T.astype(BF)

        @pl.when(j == all_steps - 1)
        def _():
            y_out[...] = y_ref[...].astype(BF)
            dx_out[...] = dx_ref[...].astype(BF)

    once = pl.Buffered(1)
    whole = lambda *shape: pl.BlockSpec(shape, lambda j, *_: (0,) * len(shape), pipeline_mode=once)

    def piece_spec(piece, where):
        index = piece[2]
        if where == 0:
            return pl.BlockSpec(piece[1], lambda j, w: index(jnp.minimum(j, steps - 1), w))
        return pl.BlockSpec(piece[1], lambda j, w: index(jnp.maximum(j - steps, 0), w))

    in_specs = [whole(block_rows, width)] * n_rows + [whole(count, width), whole(width, count), whole(count, 1)]
    in_specs += [piece_spec(piece, where) for piece, _, where in pieces]
    operands = [*rows_in, grads, grads_t, gates, *(piece[0] for piece, _, _ in pieces)]
    if groups:
        rows = width // groups + 3 * tile // 2 // groups
        grad_shape = [(groups, all_steps, rows, tile)] * 2
        grad_spec = [pl.BlockSpec((groups, 1, rows, tile), lambda j, *_: (0, j, 0, 0))] * 2
    else:
        grad_shape = [(all_steps, width, 2 * tile), (all_steps, tile, width)]
        grad_spec = [pl.BlockSpec((1,) + shape[1:], lambda j, *_: (j, 0, 0)) for shape in grad_shape]
    return pl.pallas_call(
        kernel,
        out_shape=(
            jax.ShapeDtypeStruct((count, width), BF),
            jax.ShapeDtypeStruct((count, width), BF),
            jax.ShapeDtypeStruct((count, 1), F32),
            *(jax.ShapeDtypeStruct(shape, BF) for shape in grad_shape),
        ),
        grid_spec=pltpu.PrefetchScalarGridSpec(
            num_scalar_prefetch=1,
            grid=(all_steps,),
            in_specs=in_specs,
            out_specs=[whole(count, width), whole(count, width), whole(count, 1), *grad_spec],
            scratch_shapes=[
                pltpu.VMEM((count, width), BF),
                pltpu.VMEM((width, count), BF),
                pltpu.VMEM((count, 1), F32),
                pltpu.VMEM((count, width), F32),
                pltpu.VMEM((count, width), F32),
                pltpu.VMEM((width, 2 * tile), BF),
                pltpu.VMEM((2 * tile, width), BF),
                pltpu.VMEM((tile, width), BF),
                pltpu.VMEM((width, tile), BF),
                pltpu.VMEM((count, tile), BF),
                pltpu.VMEM((count, 2 * tile), BF),
            ],
        ),
        compiler_params=pltpu.CompilerParams(vmem_limit_bytes=60 * MB),
        name="gated_mlp",
        cost_estimate=pl.CostEstimate(
            flops=9 * 2 * count * width * tile * all_steps,
            bytes_accessed=40 * MB,
            transcendentals=count * tile * all_steps,
        ),
    )(words, *operands)


def unpack(parts, shards, steps, s_steps, width):
    ctxs, groups, total, wide = parts.shape
    per = wide // shards
    r = width // shards // groups
    q = per // groups
    cols = width // wide
    tall = 2 * r + cols * q
    ff, piece = steps * wide, s_steps * per
    shapes = (
        (ctxs, groups * r, 2 * ff),
        (ctxs, steps * per, width),
        (groups * r, 2 * shards * ctxs * piece),
        (ctxs * piece, width),
    )
    if per % 128 or q % 16:
        made = parts[:, :, : (steps + s_steps) * tall].reshape(ctxs, groups, -1, tall, wide)
        d_in = made[:, :, :, : 2 * r].reshape(ctxs, groups, -1, 2, r, shards, per)
        d_out = made[:, :, :, 2 * r :].reshape(ctxs, groups, -1, cols, q, wide)
        e_in = d_in[:, :, :steps].transpose(0, 1, 4, 3, 5, 2, 6)
        e_out = d_out[:, :, :steps].transpose(0, 2, 1, 4, 3, 5)
        s_in = d_in[:, :, steps:].transpose(1, 4, 3, 5, 0, 2, 6)
        s_out = d_out[:, :, steps:].transpose(0, 2, 1, 4, 3, 5)
        return [g.astype(F32).reshape(shape) for g, shape in zip((e_in, e_out, s_in, s_out), shapes)]

    def kernel(in_ref, ein_ref, eout_ref, sin_ref, sout_ref):
        c = pl.program_id(0)

        def get(z, row, high):
            return in_ref[0, z, row : row + high, :].astype(F32)

        for z in range(groups):
            at = slice(z * r, (z + 1) * r)
            for j in range(steps):
                for g in range(2):
                    got = get(z, j * tall + g * r, r)
                    for n in range(shards):
                        col = g * ff + n * (ff // shards) + j * per
                        ein_ref[0, at, col : col + per] = got[:, n * per : (n + 1) * per]
                for b in range(cols):
                    row = j * per + z * q
                    got = get(z, j * tall + 2 * r + b * q, q)
                    eout_ref[0, row : row + q, b * wide : (b + 1) * wide] = got
            for j in range(s_steps):
                first = (steps + j) * tall
                for g in range(2):
                    got = get(z, first + g * r, r)
                    for n in range(shards):
                        col = ((g * shards + n) * ctxs + c) * piece + j * per
                        sin_ref[at, pl.ds(pl.multiple_of(col, 128), per)] = got[:, n * per : (n + 1) * per]
                for b in range(cols):
                    row = j * per + z * q
                    got = get(z, first + 2 * r + b * q, q)
                    sout_ref[row : row + q, b * wide : (b + 1) * wide] = got

    outs = pl.pallas_call(
        kernel,
        out_shape=tuple(jax.ShapeDtypeStruct(shape, F32) for shape in shapes),
        grid=(ctxs,),
        in_specs=[pl.BlockSpec((1, groups, total, wide), lambda c: (c, 0, 0, 0))],
        out_specs=(
            pl.BlockSpec((1,) + shapes[0][1:], lambda c: (c, 0, 0)),
            pl.BlockSpec((1,) + shapes[1][1:], lambda c: (c, 0, 0)),
            pl.BlockSpec(shapes[2], lambda c: (0, 0), pipeline_mode=pl.Buffered(1)),
            pl.BlockSpec((piece, width), lambda c: (c, 0)),
        ),
        compiler_params=pltpu.CompilerParams(vmem_limit_bytes=58 * MB),
        name="unpack",
        cost_estimate=pl.CostEstimate(flops=0, bytes_accessed=6 * parts.size, transcendentals=0),
    )(parts)
    return outs


def weight_pieces(
    shared_in, shared_out, expert_in, expert_out, member, core, shard, shards, ctxs, steps, s_steps, per, piece
):
    rows, width = shared_in.shape[0], shared_out.shape[1]
    ff, tile = steps * per * shards, per * shards
    s_split = shared_in.reshape(rows, 2, shards, ctxs, piece)
    pick = lambda array, who, axis: lax.dynamic_index_in_dim(array, who, axis, keepdims=False)

    if shards != 2:

        def tiles(e, s):
            gathered = []
            for v, count in ((e, steps), (s, s_steps)):
                v = v.reshape(rows, 2, shards, count, per).transpose(3, 0, 1, 2, 4).reshape(count, rows, 2 * tile)
                gathered.append(lax.all_gather(v, "fsdp", axis=1, tiled=True))
            return gathered

        e_in, s_in = tiles(pick(expert_in, member, 0), pick(s_split, member, 3))
        e_out = pick(expert_out, member, 0).reshape(steps, per, width)
        s_out = lax.dynamic_slice_in_dim(shared_out, member * piece, piece, 0).reshape(s_steps, per, width)
        e_out, s_out = (lax.all_gather(v, "fsdp", axis=1, tiled=True) for v in (e_out, s_out))
        made = [
            (
                [(v, (None, width, 2 * tile), lambda j, w: (j, 0, 0), 0, width, None, 0, 0)],
                [(o, (None, tile, width), lambda j, w: (j, 0, 0), 0, tile, None, 0, 0)],
            )
            for v, o in ((e_in, e_out), (s_in, s_out))
        ]
        return made[0], made[1], jnp.zeros((2,), jnp.int32), ((), (), ())

    who, part = member ^ 1, rows // 2
    half = width // 2
    sent = [
        lax.dynamic_slice(expert_in, (who, core * part, 0), (1, part, 2 * ff))[0],
        lax.dynamic_slice(expert_out, (who, 0, core * half), (1, expert_out.shape[1], half))[0],
        jnp.concatenate(
            [
                lax.dynamic_slice(shared_in, (core * part, ((g * shards + n) * ctxs + who) * piece), (part, piece))
                for g in range(2)
                for n in range(shards)
            ],
            axis=1,
        ),
        lax.dynamic_slice(shared_out, (who * piece, core * half), (piece, half)),
    ]
    got = [swap_with(v, "fsdp", 1) for v in sent]
    sib = [swap_with(v, "ctx", 1) for v in got]
    far_row, far_out = (1 - shard) * rows, (1 - shard) * per
    words = [
        member, core, shard * rows, far_row + core * part, far_row + (1 - core) * part,
        shard * per, far_out, core * half, (1 - core) * half,
    ]
    words = jnp.stack(words).astype(jnp.int32)
    blocks, s_blocks = ff // shards // per, piece // per
    e_ins, s_ins = [], []
    for g in range(2):
        for n in range(shards):
            lane = g * tile + n * per
            e_col = lambda j, g=g, n=n: (g * shards + n) * blocks + j
            s_own = lambda j, w, g=g, n=n: ((g * shards + n) * ctxs + w[0]) * s_blocks + j
            s_far = lambda j, g=g, n=n: (g * shards + n) * s_blocks + j
            e_own = lambda j, w, col=e_col: (w[0], 0, col(j))
            e_ins.append((expert_in, (None, rows, per), e_own, 2, 16, None, 0, lane))
            s_ins.append((shared_in, (rows, per), lambda j, w, col=s_own: (0, col(j, w)), 2, 16, None, 0, lane))
            for word, source in ((3, got), (4, sib)):
                e_ins.append((source[0], (part, per), lambda j, w, col=e_col: (0, col(j)), word, 16, None, 0, lane))
                s_ins.append((source[2], (part, per), lambda j, w, col=s_far: (0, col(j)), word, 16, None, 0, lane))
    e_outs = [(expert_out, (None, per, width), lambda j, w: (w[0], j, 0), 5, per, None, 0, 0)]
    s_outs = [(shared_out, (per, width), lambda j, w: (w[0] * s_blocks + j, 0), 5, per, None, 0, 0)]
    for word, source in ((7, got), (8, sib)):
        e_outs.append((source[1], (per, half), lambda j, w: (j, 0), 6, per, word, 128, 0))
        s_outs.append((source[3], (per, half), lambda j, w: (j, 0), 6, per, word, 128, 0))
    return (e_ins, e_outs), (s_ins, s_outs), words, (sent, got, sib)


def inverse_rms(values):
    return lax.rsqrt(jnp.mean(values * values, axis=-1, keepdims=True) + EPS)


def norm_back(values, inverse, gain, grad):
    scaled = grad * gain
    dotted = jnp.mean(scaled * values, axis=-1, keepdims=True)
    return inverse * scaled - values * (inverse * inverse * inverse) * dotted


def half_turn(pairs):
    size = pairs * HEAD_DIM
    row = lax.broadcasted_iota(jnp.int32, (size, size), 0)
    col = lax.broadcasted_iota(jnp.int32, (size, size), 1)
    return (row == (col ^ (HEAD_DIM // 2))).astype(BF)


def on_device(
    tokens,
    segment_ids,
    routes,
    cotangent,
    norm1_gain,
    qkv_weight,
    out_weight,
    norm2_gain,
    router_weight,
    shared_in,
    shared_out,
    expert_in,
    expert_out,
):
    local_len, seqs, width = tokens.shape
    count = local_len * seqs
    groups = lax.axis_size("head")
    ctxs = lax.axis_size("ctx")
    shards = lax.axis_size("fsdp")
    ctx = lax.axis_index("ctx")
    head = lax.axis_index("head")
    shard = lax.axis_index("fsdp")
    group_width = width // groups
    heads = group_width // HEAD_DIM
    block = local_len * groups
    span = seqs * block
    experts = expert_in.shape[0]
    rows_per = width // shards
    ff = expert_in.shape[2] // 2
    fs = shared_in.shape[1] // 2
    fs_part = fs // ctxs
    ctx_word = ctx.astype(jnp.int32).reshape(1)

    member = group_member()
    piece = fs // shards // ctxs
    tile = 256
    per = tile // shards
    steps, s_steps = ff // tile, fs_part // tile
    x_own = tokens.transpose(1, 0, 2)
    w_group = lax.dynamic_index_in_dim(qkv_weight.reshape(-1, 3, groups, group_width), head, 2, keepdims=False)
    w_group = fsdp_gather_small(w_group.reshape(-1, 3 * group_width), 0)
    small = jnp.concatenate([norm1_gain[None], norm2_gain[None], router_weight.T], axis=0)
    small = fsdp_gather_small(small, 1)
    x_line = line_gather_kernel(x_own, 0)
    gain_one, gain_two = small[0].astype(F32), small[1].astype(F32)
    w_router = small[2:]
    w_q, w_kv = w_group[:, :group_width], w_group[:, group_width:]
    w_q_turned = dot(w_q, half_turn(heads)).astype(BF)
    w_kv_turned = dot(w_kv, half_turn(2 * heads)).astype(BF)

    dz_own = cotangent.transpose(1, 0, 2).reshape(count, width)
    index = jnp.arange(HEAD_DIM // 2).astype(F32)
    freq = jnp.exp(-math.log(ROPE_BASE) * 2.0 * index / HEAD_DIM)
    position = ctx * block + jnp.arange(block, dtype=jnp.int32)
    angle = position.astype(F32)[:, None] * freq[None, :]
    cosine, sine = jnp.cos(angle), jnp.sin(angle)
    scale = HEAD_DIM**-0.5
    cos_q = jnp.tile(cosine, (1, 2 * heads))
    sin_q = jnp.tile(jnp.concatenate([-sine, sine], axis=1), (1, heads))
    cos_kv = jnp.concatenate([cos_q, jnp.ones_like(cos_q)], axis=1)[None]
    sin_kv = jnp.concatenate([sin_q, jnp.zeros_like(sin_q)], axis=1)[None]
    cos_q, sin_q = cos_q[None] * scale, sin_q[None] * scale

    x_f = x_line.astype(F32)
    inverse_one = inverse_rms(x_f)
    normed = (x_f * inverse_one * gain_one).astype(BF)
    normed_rows = normed.reshape(span, width)

    def turned(weight, weight_turned, cos_table, sin_table):
        plain = dot(normed_rows, weight).reshape(seqs, block, -1)
        other = dot(normed_rows, weight_turned).reshape(seqs, block, -1)
        return (plain * cos_table + other * sin_table).astype(BF)

    key_value = turned(w_kv, w_kv_turned, cos_kv, sin_kv)
    kv_blocks = ctx_gather(key_value)
    queries = turned(w_q, w_q_turned, cos_q, sin_q)
    e_pieces, s_pieces, words, sent = weight_pieces(
        shared_in, shared_out, expert_in, expert_out, after(member, corner(key_value)), ctx % 2, shard, shards, ctxs, steps, s_steps, per, piece
    )
    kv_near = jnp.stack(kv_blocks[:2])
    kv_far = jnp.stack(kv_blocks[2:])
    dz_all = jnp.concatenate(group_gather(after(dz_own, corner(key_value))), axis=0)
    w_attn = fsdp_gather_small(out_weight, 0)

    def forward_bounds(tq, tk):
        nq = block // tq
        first = ctx * block + jnp.arange(nq, dtype=jnp.int32) * tq
        low = segment_ids[:, ::tq] // tk
        last_start = segment_ids[:, tq - 1 :: tq]
        clear_to = jnp.broadcast_to(first // tk, low.shape)
        clear_from = jnp.minimum((last_start + tk - 1) // tk, clear_to)
        clear_from = jnp.maximum(clear_from, low)
        clear_to = jnp.maximum(clear_to, clear_from)
        high = jnp.broadcast_to((first + tq - 1) // tk + 1, low.shape)
        return jnp.stack([low, clear_from, clear_to, high], axis=2).astype(jnp.int32)

    fwd_q, fwd_k = min(1024, block), min(512, block)
    bounds = forward_bounds(fwd_q, fwd_k)
    near_base = (ctx // 2) * 2
    far_base = near_base ^ 2
    near_words = jnp.stack([ctx, 0 * ctx, near_base]).astype(jnp.int32)
    far_words = jnp.stack([ctx, 0 * ctx + 2, far_base]).astype(jnp.int32)
    edge = near_base * (block // fwd_k)
    starts = segment_ids[:, None, :]
    state = attend_forward(near_words, jnp.maximum(bounds, edge), queries, kv_near, starts, fwd_q, fwd_k, None)
    dz_t = dz_all.T
    state = [after(state[0], *sent[1], dz_t), state[1]]
    attended, attended_low, lse = attend_forward(
        far_words, jnp.minimum(bounds, edge), queries, kv_far, starts, fwd_q, fwd_k, state
    )
    attended_low = after(attended_low, *sent[2], w_attn)
    sent = attended_low.reshape(seqs, groups, local_len, group_width)
    back = lax.all_to_all(sent, "head", split_axis=1, concat_axis=3, tiled=True)
    attn_rows = back.reshape(count, width)

    x_rows = x_own.reshape(count, width).astype(F32)
    hidden = x_rows + dot(attn_rows, w_attn)
    inverse_two = inverse_rms(hidden)
    normed_two = (hidden * inverse_two * gain_two).astype(BF)
    route_rows = routes.reshape(local_len, seqs, 2).transpose(1, 0, 2).reshape(count, 2)
    logits = dot_t(normed_two, w_router)
    ids = jnp.arange(experts, dtype=jnp.int32)
    picks = (route_rows[:, :, None] == ids).astype(F32)
    chosen = jnp.sum(logits[:, None, :] * picks, axis=2)
    gate_first = 1.0 / (1.0 + jnp.exp(chosen[:, 1:] - chosen[:, :1]))
    gates = jnp.concatenate([gate_first, 1.0 - gate_first], axis=1)
    combine = jnp.sum(gates[:, :, None] * picks, axis=1)

    xn_blocks = group_gather(normed_two)
    combine_t = combine.T
    c_one, c_two = group_swap(combine_t, 1), group_swap(combine_t, 2)
    combine_all = jnp.concatenate([combine_t, c_one, c_two, group_swap(c_one, 2)], axis=1)
    c_own = lax.dynamic_index_in_dim(combine_all, member, 0, keepdims=False)[:, None]
    y_part, dx_part, dc, g_one, g_two = gated_mlp(
        xn_blocks, dz_all, dz_t, c_own, words, e_pieces, s_pieces, steps, s_steps, groups if paired() else 0
    )
    g_part = sum_parts(g_one, g_two)
    dc_blocks = dc.reshape(ctxs, count)
    dc_got = [
        dc_blocks[0],
        group_swap(dc_blocks[1], 1),
        group_swap(dc_blocks[2], 2),
        group_swap(group_swap(dc_blocks[3], 1), 2),
    ]
    dcombine = sum(
        dc_got[k][:, None] * ((member ^ k) == ids).astype(F32)[None, :] for k in range(ctxs)
    )
    dx_blocks = dx_part.reshape(ctxs, count, width)
    dxn2 = group_scatter([dx_blocks[k] for k in range(ctxs)])

    dchosen = jnp.sum(dcombine[:, None, :] * picks, axis=2)
    dfirst = gates[:, :1] * gates[:, 1:] * (dchosen[:, :1] - dchosen[:, 1:])
    dlogits = (dfirst * (picks[:, 0] - picks[:, 1])).astype(BF)
    router_part = dot_l(normed_two, dlogits)
    dxn2 = dxn2 + dot(dlogits, w_router)
    dz_rows = dz_own.astype(F32)
    dh = dz_rows + norm_back(hidden, inverse_two, gain_two, dxn2)
    gain_two_part = jnp.sum(dxn2 * hidden * inverse_two, axis=0)
    dh_low = dh.astype(BF)
    g_attn = dot_l(attn_rows, dh_low)
    g_attn = jnp.concatenate(
        [g_attn, gain_two_part[:, None], router_part, jnp.zeros((width, 255 - experts), F32)], axis=1
    ).astype(BF)
    dattn = dot_t(dh_low, w_attn).astype(BF).reshape(seqs, local_len, width)
    grad_out = lax.all_to_all(
        dattn.reshape(seqs, local_len, groups, group_width), "head", split_axis=2, concat_axis=1, tiled=True
    ).reshape(seqs, block, group_width)

    y_blocks = after(y_part, dh_low).reshape(ctxs, count, width)
    y_near = group_scatter_near([y_blocks[k] for k in range(ctxs)])
    grad_out = after(grad_out, *y_near)
    y_near = [y_near[0], group_swap(y_near[1], 1), group_swap(y_near[2], 2)]
    y_own = sum(v.astype(F32) for v in y_near)
    output = (hidden + y_own).astype(BF).reshape(seqs, local_len, width).transpose(1, 0, 2)

    delta = jnp.sum((grad_out.astype(F32) * attended).reshape(seqs, block, heads, HEAD_DIM), axis=3)
    stats = jnp.concatenate(
        [lse[:, :heads], delta.transpose(0, 2, 1), jnp.zeros((seqs, 8 - 2 * heads, block), F32)],
        axis=1,
    )
    tq = tk = min(512, block)
    tile_last = ctx * block + (jnp.arange(block // tq, dtype=jnp.int32) + 1) * tq - 1
    tile_key = jnp.arange(ctxs * block // tk, dtype=jnp.int32)
    q_low = jnp.sum((tile_last[None, :] < (tile_key * tk)[:, None]).astype(jnp.int32), axis=1)
    q_high = jnp.sum(((segment_ids[:, ::tq] // tk)[:, None, :] <= tile_key[None, :, None]).astype(jnp.int32), axis=2)
    q_low = jnp.broadcast_to(q_low, q_high.shape)
    back_bounds = jnp.stack([q_low, q_high], axis=2).astype(jnp.int32)
    edges = segment_ids[:, tq - 1 :: tq]
    dq_far, far_parts = attend_backward(
        far_words, back_bounds, edges, queries, kv_far, grad_out, stats, starts, tq, tk
    )
    far_sum = (far_parts[0].astype(F32) + swap_with(far_parts[1], "ctx", 1).astype(F32)).astype(BF)
    far_got = swap_with(far_sum, "ctx", 2)
    g_attn = lax.psum_scatter(g_attn, ("fsdp", "ctx"), scatter_dimension=0, tiled=True)
    g_attn = after(g_attn, corner(dq_far))
    g_attn = g_attn.reshape(-1, (width + tile) // tile, tile).transpose(1, 0, 2).reshape(-1, tile)
    whole_parts = jnp.concatenate([exchange_parts(after(g_part, corner(dq_far))), g_attn], axis=0)
    gathered = share_parts(whole_parts)
    dq_near, near_parts = attend_backward(
        near_words, back_bounds, edges, queries, kv_near, after(grad_out, corner(whole_parts), corner(far_sum)), stats, starts, tq, tk
    )
    near_parts = after(near_parts, *y_near)
    dkv = near_parts[0].astype(F32) + swap_with(near_parts[1], "ctx", 1).astype(F32) + far_got.astype(F32)
    dq = ((dq_far + dq_near) * scale).astype(BF).astype(F32)
    dkv = dkv.astype(BF).astype(F32)

    def turned_back(grad, cos_table, sin_table, pairs):
        other = (grad * sin_table).astype(BF).reshape(span, -1)
        back = dot(other, half_turn(pairs)).reshape(seqs, block, -1)
        return (grad * cos_table + back).astype(BF).reshape(span, -1)

    d_q = turned_back(dq, cos_q * HEAD_DIM**0.5, sin_q * HEAD_DIM**0.5, heads)
    d_kv = turned_back(dkv, cos_kv, sin_kv, 2 * heads)
    dxn1_part = (dot_t(d_q, w_q) + dot_t(d_kv, w_kv)).reshape(seqs, block, width)
    g_q, g_kv = dot_l(normed_rows, d_q), dot_l(normed_rows, d_kv)
    gain_one_part = jnp.sum(dxn1_part * x_f * inverse_one, axis=(0, 1))
    filler = jnp.zeros((width, 128 - 3 * group_width % 128 - 1), F32)
    g_qkv = jnp.concatenate([g_q, g_kv, gain_one_part[:, None], filler], axis=1).astype(BF)
    if paired():
        blocks = dxn1_part.astype(BF).reshape(seqs, groups, local_len, width).transpose(1, 0, 2, 3)
        dxn1, qkv_grad, side = tail_kernel(blocks.reshape(groups, count, width), g_qkv, 1)
        gain_one_grad = side[:, 3 * group_width % 128]
    else:
        dxn1 = line_scatter(dxn1_part.astype(BF), 1).reshape(count, width)
        g_qkv = lax.psum(lax.psum_scatter(g_qkv, "fsdp", scatter_dimension=0, tiled=True), "ctx")
        g_qkv = line_gather(g_qkv[:, None], 1).astype(F32)
        qkv_grad = g_qkv[..., : 3 * group_width].reshape(rows_per, groups, 3, group_width)
        qkv_grad = qkv_grad.transpose(0, 2, 1, 3).reshape(rows_per, 3 * width)
        gain_one_grad = jnp.sum(g_qkv[..., 3 * group_width], axis=1)
    dx_norm = norm_back(x_rows, inverse_rms(x_rows), gain_one, dxn1)
    tokens_grad = (dh + dx_norm).reshape(seqs, local_len, width).transpose(1, 0, 2)

    expert_in_grad, expert_out_grad, shared_in_grad, shared_out_grad = unpack(
        gathered, shards, steps, s_steps, width
    )
    g_attn = jnp.sum(gathered[:, :, (steps + s_steps) * (rows_per // groups * 2 + 3 * per // groups) :].astype(F32), axis=1)
    g_attn = g_attn.reshape(ctxs, (width + tile) // tile, -1, tile).transpose(0, 2, 1, 3).reshape(rows_per, width + tile)
    out_grad, side = g_attn[:, :width], g_attn[:, width:]
    return (
        output,
        tokens_grad,
        gain_one_grad,
        qkv_grad,
        out_grad,
        side[:, 0],
        side[:, 1 : 1 + experts],
        shared_in_grad,
        shared_out_grad,
        expert_in_grad,
        expert_out_grad,
    )


def solution(mesh):
    rows = P(("ctx", "head"), "fsdp", None)
    vector = P("fsdp")
    matrix = P("fsdp", None)
    stack = P(None, "fsdp", None)
    return jax.shard_map(
        on_device,
        mesh=mesh,
        in_specs=(
            rows,
            P("fsdp", "ctx"),
            P(("ctx", "head"), "fsdp", None, None),
            rows,
            vector,
            matrix,
            matrix,
            vector,
            matrix,
            matrix,
            matrix,
            stack,
            stack,
        ),
        out_specs=(rows, rows, vector, matrix, matrix, vector, matrix, matrix, matrix, stack, stack),
        check_vma=False,
    )
```

time: 1350 us -> 907 us (0.67)
  local copies, waits for them, and re-layouts: 422 us -> 98 us
  starting transfers between devices: 310 us -> 80.8 us
  Pallas kernels: 191 us -> 377 us
  blocking collectives: 74.9 us -> 16.5 us
  other arithmetic: 110 us -> 53.5 us
  matrix products: 22.1 us -> 37.8 us
  waiting for transfers between devices: 196 us -> 211 us
    ppermute x69 -> x1, starting transfers between devices: 187 us -> 3.58 us  [exchange_parts(): got = lax.ppermute(part, ('fsdp', 'ctx'), moves)]
    pallas_call x3 -> x6, Pallas kernels: 155 us -> 337 us  [the longest x1 125 us: tail_kernel(): pl.pallas_call(kernel, out_shape=(jax.ShapeDtypeStruct((rows, width), F32...]
    dynamic_update_slice x8 -> x0, local copies, waits for them, and re-layouts: 153 us -> none  [place(): lax.dynamic_update_slice_in_dim(out, blk.astype(F32).reshape((1,) + shape...]
    ppermute x69 -> x1, waiting for transfers between devices: 118 us -> 0.01 us  [exchange_parts(): got = lax.ppermute(part, ('fsdp', 'ctx'), moves)]
    reshape x21 -> x0, local copies, waits for them, and re-layouts: 92.9 us -> none  [the longest x16 73.7 us: place(): blk.astype(F32).reshape((1,) + shape)]
    ppermute x39 -> x41, waiting for transfers between devices: 46.1 us -> 137 us  [swap_with(): return lax.ppermute(value, axis_name, [(i, i ^ bit) for i in range(size)])]
    unnamed x6 -> x4, waiting for transfers between devices: 0.76 us -> 43.5 us
    ppermute x39 -> x41, starting transfers between devices: 116 us -> 73.6 us  [swap_with(): return lax.ppermute(value, axis_name, [(i, i ^ bit) for i in range(size)])]
  transfers between devices with their start and end apart: 116 -> 46, of which waited for: 28 -> 16; matrix products, arithmetic and copies ran while one was open for 39% -> 17% of each run, Pallas kernels for 14% -> 28%
where the time goes in v2:
time: 907 us; the launch traced here: 890 us
  Pallas kernels  377 us (42%)
  waiting for transfers between devices  211 us (23%)
  local copies, waits for them, and re-layouts  98 us (11%)
  starting transfers between devices  80.8 us (9%)
  other arithmetic  53.5 us (6%)
  matrix products  37.8 us (4%)
  blocking collectives  16.5 us (2%)
  between operations  15.8 us (2%)
    ppermute x41, waiting for transfers between devices, swap_with(): return lax.ppermute(value, axis_name, [(i, i ^ bit) for i in range(size)])  137 us
    pallas_call x1, Pallas kernels, tail_kernel(): pl.pallas_call(kernel, out_shape=(jax.ShapeDtypeStruct((rows, width), F32...  125 us
    pallas_call x1, Pallas kernels, gated_mlp(): pl.pallas_call(kernel, out_shape=(jax.ShapeDtypeStruct((count, width), BF...  107 us
    ppermute x41, starting transfers between devices, swap_with(): return lax.ppermute(value, axis_name, [(i, i ^ bit) for i in range(size)])  73.6 us
    pallas_call x1, Pallas kernels, line_gather_kernel(): pl.pallas_call(kernel, out_shape=jax.ShapeDtypeStruct((seqs, count * rows...  52.7 us
    unnamed x4, waiting for transfers between devices  43.5 us
    pallas_call x2, Pallas kernels, attend_backward(): pl.pallas_call(kernel, out_shape=(jax.ShapeDtypeStruct((seqs, rows, width...  40.4 us
    dot_general x8, matrix products, dot(): return jnp.dot(a, b, preferred_element_type=F32)  28.2 us
  transfers between devices with their start and end apart: 46, of which 16 were waited for; matrix products, arithmetic and copies ran while one was open for 17% of the time, Pallas kernels for 28%

profile of v2, /device:TPU:1, one launch (start us, length us, event | category | flops | bytes accessed | tf_op | source)
XLA Modules:
  0.0 890.0 jit_solution(11673154154651959046)
XLA Ops:
  16.9 52.7 %line_gather.1 = bf16[2,1024,768]{2,1,0:T(8,128)(2,1)S(1)} custom-call(bf16[2,256,768]{2,1,0:T(8,128)(2,1)S(1)} %bitcast.182), custom_call_target="tpu_custom_call" | custom-call | bytes 188743680 | tf_op jit(solution)/shard_map/line_gather/pallas_call | solution.py:287
  99.3 6.6 add_convert_fusion.1
  117.1 5.0 collective-permute-done.10
  134.8 32.3 %collective-permute-done.8.refs_35_ = bf16[256,384]{1,0:T(8,128)(2,1)S(1)} collective-permute-done((bf16[256,384]{1,0:T(8,128)(2,1)S(1)}, bf16[256,384]{1,0:T(8,128)(2,1)S(1)}, u32[]{:S(2)}, u32[]{:S(2)}) %collective-permute-start.8) | collective-permute-done | bytes 196640 | tf_op jit(solution)/shard_map/ppermute | solution.py:22
  177.8 11.3 %collective-permute-start.3 = (bf16[2,1024,384]{2,1,0:T(8,128)(2,1)}, bf16[2,1024,384]{2,1,0:T(8,128)(2,1)S(1)}, u32[]{:S(2)}, u32[]{:S(2)}) collective-permute-start(bf16[2,1024,384]{2,1,0:T(8,128)(2,1)} %collective-permute-done.2), channel_id=1, source_target_pairs={{0,4},{4,0},{8,12},{12,8},{1,5},{5,1},{9,13},{13,9},{2,6},{6,2},{1... | collective-permute-start | bytes 4718600 | tf_op jit(solution)/shard_map/ppermute | solution.py:22
  191.5 7.5 collective-permute-start.16
  201.5 23.3 %attend_forward.2 = (f32[2,192,1024]{2,1,0:T(8,128)S(1)}, f32[2,8,1024]{2,1,0:T(8,128)S(1)}) custom-call(s32[3]{0:T(128)S(1)} %pad_add_fusion.2.word_ref, s32[2,1,4]{2,1,0:T(1,128)S(1)} %get-tuple-element.160.bounds_ref, bf16[2,1024,192]{2,1,0:T(8,128)(2,1)S(1)} %copy-done.10, bf16[2,2,1024,384]{3,2,1,0:T(8,128)(2,1)S(1)} %pad_maximum_fusion.1.kv_ref, ...), custom_call_target="tpu_custom_call" | custom-call | flops 12884901888 | bytes 67108864 | tf_op jit(solution)/shard_map/attend_forward/pallas_call | solution.py:547
  237.3 16.5 %all_to_all.30 = bf16[2,4,256,192]{2,0,3,1:T(2,128)(2,1)S(1)} all-to-all(bf16[2,4,256,192]{2,0,3,1:T(2,128)(2,1)} %copy.254), channel_id=1, replica_groups=mesh['fsdp'=2,'ctx'=4,'head'=4] {'head'}, dimensions={1} | all-to-all | bytes 1572864 | tf_op jit(solution)/shard_map/all_to_all | solution.py:1098
  257.6 16.7 %collective-permute-start.19 = (bf16[512,768]{1,0:T(8,128)(2,1)S(1)}, bf16[512,768]{1,0:T(8,128)(2,1)}, u32[]{:S(2)}, u32[]{:S(2)}) collective-permute-start(bf16[512,768]{1,0:T(8,128)(2,1)S(1)} %multiply_convert_fusion.1.refs_0_), channel_id=1, source_target_pairs={{0,8},{4,12},{8,0},{12,4},{1,9},{5,13},{9,1},{13,5},{2,10},{6,14},... | collective-permute-start | bytes 2359304 | tf_op jit(solution)/shard_map/ppermute | solution.py:22
  279.4 12.0 %collective-permute-done.19.refs_2_ = bf16[512,768]{1,0:T(8,128)(2,1)} collective-permute-done((bf16[512,768]{1,0:T(8,128)(2,1)S(1)}, bf16[512,768]{1,0:T(8,128)(2,1)}, u32[]{:S(2)}, u32[]{:S(2)}) %collective-permute-start.19) | collective-permute-done | bytes 786464 | tf_op jit(solution)/shard_map/ppermute | solution.py:22
  301.6 5.7 collective-permute-done.22
  316.7 107.0 %gated_mlp.1 = (bf16[2048,768]{1,0:T(8,128)(2,1)}, bf16[2048,768]{1,0:T(8,128)(2,1)}, f32[2048,1]{1,0:T(8,128)}, bf16[4,10,288,256]{3,2,1,0:T(8,128)(2,1)}, bf16[4,10,288,256]{3,2,1,0:T(8,128)(2,1)}) custom-call(s32[9]{0:T(128)} %stack.106.word_ref, bf16[512,768]{1,0:T(8,128)(2,1)} %copy-done.20, bf16[512,768]{1,0:T(8,128)(2,1)} %collective-permute-done.18.refs_1_, ...), custom_call_target="tpu_custom_call" | custom-call | flops 72477573120 | bytes 41943040 | tf_op jit(solution)/shard_map/gated_mlp/pallas_call | solution.py:784
  425.8 9.4 %collective-permute-done.40 = bf16[4,10,288,256]{3,2,1,0:T(8,128)(2,1)S(1)} collective-permute-done((bf16[4,10,288,256]{3,2,1,0:T(8,128)(2,1)}, bf16[4,10,288,256]{3,2,1,0:T(8,128)(2,1)S(1)}, u32[]{:S(2)}, u32[]{:S(2)}) %collective-permute-start.40) | collective-permute-done | bytes 5898272 | tf_op jit(solution)/shard_map/ppermute | solution.py:22
  435.3 7.5 add_convert_fusion
  452.3 6.9 collective-permute-done.30
  462.6 16.1 %collective-permute-done.28 = bf16[512,768]{1,0:T(8,128)(2,1)S(1)} collective-permute-done((bf16[512,768]{1,0:T(8,128)(2,1)S(1)}, bf16[512,768]{1,0:T(8,128)(2,1)S(1)}, u32[]{:S(2)}, u32[]{:S(2)}) %collective-permute-start.28) | collective-permute-done | bytes 786464 | tf_op jit(solution)/shard_map/ppermute | solution.py:22
  508.9 24.6 %all-to-all-done.1 = bf16[2,256,4,192]{1,0,3,2:T(2,128)(2,1)S(1)} async-done(((bf16[2,256,4,192]{1,0,3,2:T(2,128)(2,1)}), bf16[2,256,4,192]{1,0,3,2:T(2,128)(2,1)S(1)}, u32[]{:S(2)}, u32[]{:S(2)}) %all-to-all-start.1) | async-done | bytes 786464 | tf_op jit(solution)/shard_map/all_to_all | solution.py:1150
  543.0 7.9 attend_backward.2
  552.2 5.6 reduce-scatter.5.cloned.1.call-done
  561.5 43.5 %reduce-scatter.7.cloned.1.call-done = bf16[96,1024]{1,0:T(8,128)(2,1)} async-done(((bf16[768,1024]{1,0:T(8,128)(2,1)}), bf16[96,1024]{1,0:T(8,128)(2,1)}) %reduce-scatter.7.cloned.1.call-update) | async-done | bytes 196624
  615.4 32.4 %attend_backward.3 = (f32[2,1024,192]{2,1,0:T(8,128)S(1)}, bf16[2,2,1024,384]{3,2,1,0:T(8,128)(2,1)}) custom-call(s32[3]{0:T(128)S(1)} %copy-done.9, s32[2,8,2]{2,1,0:T(8,128)S(1)} %pad_add_fusion.bounds_ref, s32[2,2]{1,0:T(2,128)S(1)} %slice.229.edges_ref, bf16[2,1024,192]{2,1,0:T(8,128)(2,1)S(1)} %copy-done.11, bf16[2,2,1024,384]{3,2,1,0:T(8,128)(2,1)} %copy-done.2, ...), custom_call_target="tpu_custom_call" | custom-call | flops 32212254720 | bytes 104857600 | tf_op jit(solution)/shard_map/attend_backward/pallas_call | solution.py:631
  663.8 42.2 %collective-permute-done.39 = bf16[2,1024,384]{2,1,0:T(8,128)(2,1)} collective-permute-done((bf16[2,1024,384]{2,1,0:T(8,128)(2,1)}, bf16[2,1024,384]{2,1,0:T(8,128)(2,1)}, u32[]{:S(2)}, u32[]{:S(2)}) %collective-permute-start.39) | collective-permute-done | bytes 1572896 | tf_op jit(solution)/shard_map/ppermute | solution.py:22
  717.8 125.2 %tail.1 = (f32[512,768]{1,0:T(8,128)S(1)}, f32[384,2304]{1,0:T(8,128)S(1)}, f32[384,128]{1,0:T(8,128)S(1)}) custom-call(bf16[4,512,768]{2,1,0:T(8,128)(2,1)S(1)} %bitcast.178, bf16[768,640]{1,0:T(8,128)(2,1)S(1)} %maximum_maximum_fusion.1.g_ref), custom_call_target="tpu_custom_call" | custom-call | bytes 230686720 | tf_op jit(solution)/shard_map/tail/pallas_call | solution.py:436
  854.6 25.1 %unpack.1 = (f32[4,384,4096]{2,1,0:T(8,128)}, f32[4,1024,768]{2,1,0:T(8,128)}, f32[384,4096]{1,0:T(8,128)}, f32[1024,768]{1,0:T(8,128)}) custom-call(bf16[4,4,3264,256]{3,2,1,0:T(8,128)(2,1)} %bitcast.186), custom_call_target="tpu_custom_call" | custom-call | bytes 80216064 | tf_op jit(solution)/shard_map/unpack/pallas_call | solution.py:875
  (367 shorter events, 231.5 us)
Async XLA Ops:
  7.2 550.7 %reduce-scatter.5.cloned.1.call-start = ((), (), s32[]{:S(2)}) async-start(), calls=%async_computation.4 | async-start | bytes 7372800 | tf_op jit(solution)/shard_map/reduce_scatter | solution.py:157
  9.3 83.8 %collective-permute-start = (bf16[6,384]{1,0:T(8,128)(2,1)S(1)}, bf16[6,384]{1,0:T(8,128)(2,1)S(1)}, u32[]{:S(2)}, u32[]{:S(2)}) collective-permute-start(bf16[6,384]{1,0:T(8,128)(2,1)S(1)} %pad_maximum_fusion.10), channel_id=1, source_target_pairs={{0,16},{16,0},{1,17},{17,1},{2,18},{18,2},{3,19},{19,3},{4,20},{20... | collective-permute-start | bytes 13832 | tf_op jit(solution)/shard_map/ppermute | solution.py:22
  11.4 112.8 %collective-permute-start.17 = (bf16[384,768]{1,0:T(8,128)(2,1)}, bf16[384,768]{1,0:T(8,128)(2,1)}, u32[]{:S(2)}, u32[]{:S(2)}) collective-permute-start(bf16[384,768]{1,0:T(8,128)(2,1)} %param.19), channel_id=1, source_target_pairs={{0,16},{16,0},{1,17},{17,1},{2,18},{18,2},{3,19},{19,3},{4,20},{20... | collective-permute-start | bytes 1769480 | tf_op jit(solution)/shard_map/ppermute | solution.py:22
  15.1 78.1 %collective-permute-start.1 = (bf16[384,576]{0,1:T(8,128)(2,1)}, bf16[384,576]{0,1:T(8,128)(2,1)}, u32[]{:S(2)}, u32[]{:S(2)}) collective-permute-start(bf16[384,576]{0,1:T(8,128)(2,1)} %bitcast.12), channel_id=1, source_target_pairs={{0,16},{16,0},{1,17},{17,1},{2,18},{18,2},{3,19},{19,3},{4,20},{20... | collective-permute-start | bytes 1327112 | tf_op jit(solution)/shard_map/ppermute | solution.py:22
  107.3 92.2 %collective-permute-start.4 = (bf16[2,1024,384]{2,1,0:T(8,128)(2,1)}, bf16[2,1024,384]{2,1,0:T(8,128)(2,1)}, u32[]{:S(2)}, u32[]{:S(2)}) collective-permute-start(bf16[2,1024,384]{2,1,0:T(8,128)(2,1)} %add_convert_fusion.1), channel_id=1, source_target_pairs={{0,4},{4,0},{8,12},{12,8},{1,5},{5,1},{9,13},{13,9},{2,6},{6,2},{1... | collective-permute-start | bytes 4718600 | tf_op jit(solution)/shard_map/ppermute | solution.py:22
  110.8 67.0 %collective-permute-start.2 = (bf16[2,1024,384]{2,1,0:T(8,128)(2,1)}, bf16[2,1024,384]{2,1,0:T(8,128)(2,1)}, u32[]{:S(2)}, u32[]{:S(2)}) collective-permute-start(bf16[2,1024,384]{2,1,0:T(8,128)(2,1)} %add_convert_fusion.1), channel_id=1, source_target_pairs={{0,8},{4,12},{8,0},{12,4},{1,9},{5,13},{9,1},{13,5},{2,10},{6,14},... | collective-permute-start | bytes 4718600 | tf_op jit(solution)/shard_map/ppermute | solution.py:22
  122.2 76.9 %collective-permute-start.5 = (bf16[192,4096]{1,0:T(8,128)(2,1)}, bf16[192,4096]{1,0:T(8,128)(2,1)}, u32[]{:S(2)}, u32[]{:S(2)}) collective-permute-start(bf16[192,4096]{1,0:T(8,128)(2,1)} %dynamic-slice_bitcast_fusion), channel_id=1, source_target_pairs={{0,16},{16,0},{1,17},{17,1},{2,18},{18,2},{3,19},{19,3},{4,20},{20... | collective-permute-start | bytes 4718600 | tf_op jit(solution)/shard_map/ppermute | solution.py:22
  124.2 43.1 %collective-permute-start.12 = (bf16[256,768]{1,0:T(8,128)(2,1)}, bf16[256,768]{1,0:T(8,128)(2,1)}, u32[]{:S(2)}, u32[]{:S(2)}) collective-permute-start(bf16[256,768]{1,0:T(8,128)(2,1)} %slice.246), channel_id=1, source_target_pairs={{0,16},{16,0},{1,17},{17,1},{2,18},{18,2},{3,19},{19,3},{4,20},{20... | collective-permute-start | bytes 1179656 | tf_op jit(solution)/shard_map/ppermute | solution.py:22
  131.1 35.9 %collective-permute-start.8 = (bf16[256,384]{1,0:T(8,128)(2,1)S(1)}, bf16[256,384]{1,0:T(8,128)(2,1)S(1)}, u32[]{:S(2)}, u32[]{:S(2)}) collective-permute-start(bf16[256,384]{1,0:T(8,128)(2,1)S(1)} %dynamic_slice.36), channel_id=1, source_target_pairs={{0,16},{16,0},{1,17},{17,1},{2,18},{18,2},{3,19},{19,3},{4,20},{20... | collective-permute-start | bytes 589832 | tf_op jit(solution)/shard_map/ppermute | solution.py:22
  167.1 31.9 %collective-permute-start.6 = (bf16[1024,384]{1,0:T(8,128)(2,1)S(1)}, bf16[1024,384]{1,0:T(8,128)(2,1)S(1)}, u32[]{:S(2)}, u32[]{:S(2)}) collective-permute-start(bf16[1024,384]{1,0:T(8,128)(2,1)S(1)} %dynamic-slice_bitcast_fusion.1), channel_id=1, source_target_pairs={{0,16},{16,0},{1,17},{17,1},{2,18},{18,2},{3,19},{19,3},{4,20},{20... | collective-permute-start | bytes 2359304 | tf_op jit(solution)/shard_map/ppermute | solution.py:22
  177.8 46.9 %collective-permute-start.3 = (bf16[2,1024,384]{2,1,0:T(8,128)(2,1)}, bf16[2,1024,384]{2,1,0:T(8,128)(2,1)S(1)}, u32[]{:S(2)}, u32[]{:S(2)}) collective-permute-start(bf16[2,1024,384]{2,1,0:T(8,128)(2,1)} %collective-permute-done.2), channel_id=1, source_target_pairs={{0,4},{4,0},{8,12},{12,8},{1,5},{5,1},{9,13},{13,9},{2,6},{6,2},{1... | collective-permute-start | bytes 4718600 | tf_op jit(solution)/shard_map/ppermute | solution.py:22
  191.5 41.2 %collective-permute-start.16 = (bf16[256,384]{1,0:T(8,128)(2,1)S(1)}, bf16[256,384]{1,0:T(8,128)(2,1)S(1)}, u32[]{:S(2)}, u32[]{:S(2)}) collective-permute-start(bf16[256,384]{1,0:T(8,128)(2,1)S(1)} %collective-permute-done.8.refs_35_), channel_id=1, source_target_pairs={{0,4},{4,0},{8,12},{12,8},{1,5},{5,1},{9,13},{13,9},{2,6},{6,2},{1... | collective-permute-start | bytes 589832 | tf_op jit(solution)/shard_map/ppermute | solution.py:22
  199.0 33.8 %collective-permute-start.15 = (bf16[192,1024]{1,0:T(8,128)(2,1)}, bf16[192,1024]{1,0:T(8,128)(2,1)}, u32[]{:S(2)}, u32[]{:S(2)}) collective-permute-start(bf16[192,1024]{1,0:T(8,128)(2,1)} %collective-permute-done.7.refs_23_.refs_26_.refs_29_.refs_32_), channel_id=1, source_target_pairs={{0,4},{4,0},{8,12},{12,8},{1,5},{5,1},{9,13},{13,9},{2,6},{6,2},{1... | collective-permute-start | bytes 1179656 | tf_op jit(solution)/shard_map/ppermute | solution.py:22
  199.0 33.7 %collective-permute-start.14 = (bf16[1024,384]{1,0:T(8,128)(2,1)S(1)}, bf16[1024,384]{1,0:T(8,128)(2,1)S(1)}, u32[]{:S(2)}, u32[]{:S(2)}) collective-permute-start(bf16[1024,384]{1,0:T(8,128)(2,1)S(1)} %collective-permute-done.6.refs_20_), channel_id=1, source_target_pairs={{0,4},{4,0},{8,12},{12,8},{1,5},{5,1},{9,13},{13,9},{2,6},{6,2},{1... | collective-permute-start | bytes 2359304 | tf_op jit(solution)/shard_map/ppermute | solution.py:22
  199.5 33.3 %collective-permute-start.13 = (bf16[192,4096]{1,0:T(8,128)(2,1)}, bf16[192,4096]{1,0:T(8,128)(2,1)}, u32[]{:S(2)}, u32[]{:S(2)}) collective-permute-start(bf16[192,4096]{1,0:T(8,128)(2,1)} %collective-permute-done.5.refs_8_.refs_11_.refs_14_.refs_17_), channel_id=1, source_target_pairs={{0,4},{4,0},{8,12},{12,8},{1,5},{5,1},{9,13},{13,9},{2,6},{6,2},{1... | collective-permute-start | bytes 4718600 | tf_op jit(solution)/shard_map/ppermute | solution.py:22
  257.6 33.8 %collective-permute-start.19 = (bf16[512,768]{1,0:T(8,128)(2,1)S(1)}, bf16[512,768]{1,0:T(8,128)(2,1)}, u32[]{:S(2)}, u32[]{:S(2)}) collective-permute-start(bf16[512,768]{1,0:T(8,128)(2,1)S(1)} %multiply_convert_fusion.1.refs_0_), channel_id=1, source_target_pairs={{0,8},{4,12},{8,0},{12,4},{1,9},{5,13},{9,1},{13,5},{2,10},{6,14},... | collective-permute-start | bytes 2359304 | tf_op jit(solution)/shard_map/ppermute | solution.py:22
  489.5 44.0 %all-to-all-start.1 = ((bf16[2,256,4,192]{1,0,3,2:T(2,128)(2,1)}), bf16[2,256,4,192]{1,0,3,2:T(2,128)(2,1)S(1)}, u32[]{:S(2)}, u32[]{:S(2)}) async-start(bf16[2,256,4,192]{1,0,3,2:T(2,128)(2,1)} %reshape_reshape.6), calls=%async_computation.1 | async-start | bytes 1572864 | tf_op jit(solution)/shard_map/all_to_all | solution.py:1150
  493.0 111.9 %reduce-scatter.7.cloned.1.call-start = ((), (), s32[]{:S(2)}) async-start(), calls=%async_computation.6 | async-start | bytes 1769472
  502.5 345.6 %all-gather.3.cloned.1.call-start = ((), (), s32[]{:S(2)}) async-start(), calls=%async_computation.5 | async-start | bytes 28409856 | tf_op jit(solution)/shard_map/all_gather | solution.py:171
  557.9 48.3 %collective-permute-start.41 = (bf16[2880,256]{1,0:T(8,128)(2,1)}, bf16[2880,256]{1,0:T(8,128)(2,1)}, u32[]{:S(2)}, u32[]{:S(2)}) collective-permute-start(bf16[2880,256]{1,0:T(8,128)(2,1)} %reduce-scatter.5.cloned.1.call-done), channel_id=1, source_target_pairs={{4,16},{12,24},{16,4},{24,12},{5,17},{13,25},{17,5},{25,13},{6,18}... | collective-permute-start | bytes 4423688 | tf_op jit(solution)/shard_map/ppermute | solution.py:166
  610.0 37.9 %collective-permute-start.36 = (bf16[512,768]{1,0:T(8,128)(2,1)}, bf16[512,768]{1,0:T(8,128)(2,1)S(1)}, u32[]{:S(2)}, u32[]{:S(2)}) collective-permute-start(bf16[512,768]{1,0:T(8,128)(2,1)} %pad_maximum_fusion.7), channel_id=1, source_target_pairs={{0,8},{4,12},{8,0},{12,4},{1,9},{5,13},{9,1},{13,5},{2,10},{6,14},... | collective-permute-start | bytes 2359304 | tf_op jit(solution)/shard_map/ppermute | solution.py:22
  612.5 35.4 %collective-permute-start.34 = (bf16[512,768]{1,0:T(8,128)(2,1)}, bf16[512,768]{1,0:T(8,128)(2,1)S(1)}, u32[]{:S(2)}, u32[]{:S(2)}) collective-permute-start(bf16[512,768]{1,0:T(8,128)(2,1)} %pad_maximum_fusion.6), channel_id=1, source_target_pairs={{0,16},{16,0},{1,17},{17,1},{2,18},{18,2},{3,19},{19,3},{4,20},{20... | collective-permute-start | bytes 2359304 | tf_op jit(solution)/shard_map/ppermute | solution.py:22
  614.4 37.0 %collective-permute-start.38 = (bf16[2,1024,384]{2,1,0:T(8,128)(2,1)S(1)}, bf16[2,1024,384]{2,1,0:T(8,128)(2,1)S(1)}, u32[]{:S(2)}, u32[]{:S(2)}) collective-permute-start(bf16[2,1024,384]{2,1,0:T(8,128)(2,1)S(1)} %slice_bitcast_fusion), channel_id=1, source_target_pairs={{0,4},{4,0},{8,12},{12,8},{1,5},{5,1},{9,13},{13,9},{2,6},{6,2},{1... | collective-permute-start | bytes 4718600 | tf_op jit(solution)/shard_map/ppermute | solution.py:22
  652.9 53.1 %collective-permute-start.39 = (bf16[2,1024,384]{2,1,0:T(8,128)(2,1)}, bf16[2,1024,384]{2,1,0:T(8,128)(2,1)}, u32[]{:S(2)}, u32[]{:S(2)}) collective-permute-start(bf16[2,1024,384]{2,1,0:T(8,128)(2,1)} %fusion.8), channel_id=1, source_target_pairs={{0,8},{4,12},{8,0},{12,4},{1,9},{5,13},{9,1},{13,5},{2,10},{6,14},... | collective-permute-start | bytes 4718600 | tf_op jit(solution)/shard_map/ppermute | solution.py:22
  (85 other events, 1473.9 us)
Sparse Core Ops, SparseCore 0:
  442.9 114.9 reduce-scatter.4
  561.2 43.7 reduce-scatter.6
  609.2 232.2 all-gather.2
